TPU v7x, 32 devices: a whole 2x2x4 slice. The times are simulated.
32 devices in a mesh: dp: 4 (over y, x), seq: 8 (over z, core).
Axes of the slice: x: 2, y: 2, z: 4, core: 2. Of those that a mesh axis runs over, the one named last changes fastest.
Arguments:
- tokens: bfloat16 [8, 1024, 1024], P('dp', 'seq'), may hold values from -7 to 7
- cotangent: bfloat16 [8, 1024, 1024], P('dp', 'seq'), may hold values from -6 to 6
- starts: int32 [8, 4], P('dp'), may hold values from 0 to 768, as said below
- mixer_gain: bfloat16 [1, 1024], P(None, ('dp', 'seq')), may hold values from 0.5 to 1.5
- mix_weight: bfloat16 [1, 1024, 4096], P(None, ('dp', 'seq')), may hold values from -0.1875 to 0.1875
- conv_weight: bfloat16 [1, 4, 3072], P(None, None, ('dp', 'seq')), may hold values from -3 to 3
- beta_weight: bfloat16 [1, 1024, 8], P(None, ('dp', 'seq')), may hold values from -0.5 to 0.5
- head_gain: bfloat16 [1, 128], replicated, may hold values from 0.5 to 1.5
- out_weight: bfloat16 [1, 1024, 1024], P(None, ('dp', 'seq')), may hold values from -0.1875 to 0.1875
- mlp_gain: bfloat16 [1, 1024], P(None, ('dp', 'seq')), may hold values from 0.5 to 1.5
- upgate_weight: bfloat16 [1, 1024, 5632], P(None, ('dp', 'seq')), may hold values from -0.1875 to 0.1875
- down_weight: bfloat16 [1, 2816, 1024], P(None, ('dp', 'seq')), may hold values from -0.109375 to 0.109375
Outputs:
- output: bfloat16 [8, 1024, 1024], P('dp', 'seq')
- input_grad: float32 [8, 1024, 1024], P('dp', 'seq')
- mixer_gain_grad: float32 [1, 1024], P(None, ('dp', 'seq'))
- mix_weight_grad: float32 [1, 1024, 4096], P(None, ('dp', 'seq'))
- conv_weight_grad: float32 [1, 4, 3072], P(None, None, ('dp', 'seq'))
- beta_weight_grad: float32 [1, 1024, 8], P(None, ('dp', 'seq'))
- head_gain_grad: float32 [1, 128], replicated
- out_weight_grad: float32 [1, 1024, 1024], P(None, ('dp', 'seq'))
- mlp_gain_grad: float32 [1, 1024], P(None, ('dp', 'seq'))
- upgate_weight_grad: float32 [1, 1024, 5632], P(None, ('dp', 'seq'))
- down_weight_grad: float32 [1, 2816, 1024], P(None, ('dp', 'seq'))
Inputs may be any that keep to these rules, and one draw needn't show every extreme that they name: `starts`: entries are multiples of 64, and each row's first entry is 0. Rows come in groups of 2 consecutive rows; in two groups one row packs 4 sequences whose increasing start positions are its entries, the last at 768; every other row holds one sequence and has all entries 0.
All inputs are finite; a program needn't handle non-finite values.
Results may differ from a plain program's by a relative error of at most 0.015.
Values may be sent and summed in bfloat16 or wider, within the bound.
A program may use at most 256 MiB of HBM per device.

v0:
```python
import jax
import jax.numpy as jnp
from jax import lax
from jax.sharding import PartitionSpec as P

MODEL_WIDTH = 1024
HEADS = 8
HEAD_SIZE = 128
FF = 2816
KW = 4
BLOCK_TOKENS = 64
LAYERS = 1


small_block = 1e-06
small_head = 1e-05
exact = lax.Precision.HIGHEST


def from_behind(value, axis, steps):
    count = lax.axis_size(axis)
    initial, last = (max(0, -steps), min(count, count - steps))
    return lax.ppermute(value, axis, [(source, source + steps) for source in range(initial, last)])


def segment_of(starts, token_places):
    live = starts > 0
    hits = live[:, None, :] & (starts[:, None, :] <= token_places[None, :, None])
    return jnp.sum(hits.astype(jnp.int32), axis=-1)


def make_taps(starts, token_places):
    current = segment_of(starts, token_places)
    listed = []
    for shift_by in range(KW):
        source = token_places - shift_by
        valid = (source[None, :] >= 0) & (segment_of(starts, source) == current)
        listed.append(valid.astype(jnp.float32))
    return jnp.stack(listed)


def build_kept_masks(starts, begins):
    hit = jnp.any((starts[:, None, :] == begins[None, :, None]) & (starts[:, None, :] > 0), axis=-1)
    return 1.0 - hit.astype(jnp.float32)


def convolve(padded, weight, taps, length):
    total = jnp.zeros((padded.shape[0], length, padded.shape[2]), jnp.float32)
    for shift_by in range(KW):
        begin = KW - 1 - shift_by
        total = (
            total + weight[shift_by] * padded[:, begin : begin + length] * taps[shift_by][..., None]
        )
    return total


def head_inputs(active, betas, rows, count):

    def arrange(part):
        return part.reshape(rows, count, BLOCK_TOKENS, HEADS, HEAD_SIZE).transpose(1, 0, 3, 2, 4)

    def unit(part):
        split = part.reshape(part.shape[0], part.shape[1], HEADS, HEAD_SIZE)
        scaled = split * lax.rsqrt(jnp.sum(split * split, axis=-1, keepdims=True) + 1e-06)
        return scaled.reshape(part.shape)

    queries = arrange(unit(active[..., :MODEL_WIDTH]) * HEAD_SIZE ** (-0.5))
    keys_in = arrange(unit(active[..., MODEL_WIDTH : 2 * MODEL_WIDTH]))
    values = arrange(active[..., 2 * MODEL_WIDTH :])
    betas_h = betas.reshape(rows, count, BLOCK_TOKENS, HEADS).transpose(1, 0, 3, 2)
    return (queries, keys_in, values, betas_h)


def block_parts(queries, keys_in, values, betas_h):
    size = keys_in.shape[-2]
    lower = jnp.tril(jnp.ones((size, size), jnp.float32), -1)
    within = jnp.tril(jnp.ones((size, size), jnp.float32))
    weighted = betas_h[..., None]
    gram = jnp.einsum("...ik,...jk->...ij", keys_in, keys_in, precision=exact)
    system = jnp.eye(size, dtype=jnp.float32) + lower * weighted * gram
    solved_w = jax.scipy.linalg.solve_triangular(
        system, weighted * keys_in, lower=True, unit_diagonal=True
    )
    solved_u = jax.scipy.linalg.solve_triangular(
        system, weighted * values, lower=True, unit_diagonal=True
    )
    attend = within * jnp.einsum("...ik,...jk->...ij", queries, keys_in, precision=exact)
    return (solved_w, solved_u, attend)


def block_step(state, inputs):
    queries, keys_in, solved_w, solved_u, attend, keep = inputs
    state = keep[:, None, None, None] * state
    fresh = solved_u - jnp.einsum("rhck,rhkv->rhcv", solved_w, state, precision=exact)
    output = jnp.einsum("rhck,rhkv->rhcv", queries, state, precision=exact)
    output = output + jnp.einsum("rhij,rhjv->rhiv", attend, fresh, precision=exact)
    state = state + jnp.einsum("rhck,rhcv->rhkv", keys_in, fresh, precision=exact)
    return (state, output)


def transition_step(carry, inputs):
    power, offset_s = carry
    keys_in, solved_w, solved_u, keep = inputs
    scale = keep[:, None, None, None]
    power = scale * power
    offset_s = scale * offset_s
    moved = jnp.einsum("rhcj,rhjm->rhcm", solved_w, power, precision=exact)
    power = power - jnp.einsum("rhck,rhcm->rhkm", keys_in, moved, precision=exact)
    fresh = solved_u - jnp.einsum("rhcj,rhjv->rhcv", solved_w, offset_s, precision=exact)
    offset_s = offset_s + jnp.einsum("rhck,rhcv->rhkv", keys_in, fresh, precision=exact)
    return ((power, offset_s), None)


def compose(earlier, later):
    return (
        jnp.einsum("rhij,rhjk->rhik", later[0], earlier[0], precision=exact),
        jnp.einsum("rhij,rhjk->rhik", later[0], earlier[1], precision=exact) + later[1],
    )


def compose_stacked(earlier, later):
    joined = compose((earlier[0], earlier[1]), (later[0], later[1]))
    return jnp.stack(joined)


def identity_stacked(shape):
    return jnp.stack(
        [
            jnp.broadcast_to(jnp.eye(HEAD_SIZE, dtype=jnp.float32), shape),
            jnp.zeros(shape, jnp.float32),
        ]
    )


def forward_doubling(pair):
    count = lax.axis_size("seq")
    index = lax.axis_index("seq")
    current = jnp.stack(pair)
    neutral = identity_stacked(pair[0].shape)
    distances = [1]
    reach_now = 1
    while reach_now < count:
        distances.append(reach_now)
        reach_now = reach_now * 2
    for turn, distance in enumerate(distances):
        arrived = from_behind(current.astype(jnp.bfloat16), "seq", distance).astype(current.dtype)
        arrived = jnp.where(index >= distance, arrived, neutral)
        current = arrived if turn == 0 else compose_stacked(arrived, current)
    return (current[0], current[1])


def backward_doubling(pair):
    count = lax.axis_size("seq")
    index = lax.axis_index("seq")
    current = jnp.stack(pair)
    neutral = identity_stacked(pair[0].shape)
    distances = [1]
    reach_now = 1
    while reach_now < count:
        distances.append(reach_now)
        reach_now = reach_now * 2
    for turn, distance in enumerate(distances):
        arrived = from_behind(current.astype(jnp.bfloat16), "seq", -distance).astype(current.dtype)
        arrived = jnp.where(index + distance <= count - 1, arrived, neutral)
        current = arrived if turn == 0 else compose_stacked(arrived, current)
    return (current[0], current[1])


def make_parts(active, betas):
    rows = active.shape[0]
    count = active.shape[1] // BLOCK_TOKENS
    queries, keys_in, values, betas_h = head_inputs(active, betas, rows, count)
    solved_w, solved_u, attend = block_parts(queries, keys_in, values, betas_h)
    return (queries, keys_in, solved_w, solved_u, attend)


def apply_parts(parts, state_in, kept_masks):
    queries, keys_in, solved_w, solved_u, attend = parts
    state_out, outputs = lax.scan(
        block_step, state_in, (queries, keys_in, solved_w, solved_u, attend, kept_masks)
    )
    count, rows = (outputs.shape[0], outputs.shape[1])
    return (
        outputs.transpose(1, 0, 3, 2, 4).reshape(rows, count * BLOCK_TOKENS, MODEL_WIDTH),
        state_out,
    )


def transition(parts, kept_masks):
    queries, keys_in, solved_w, solved_u, attend = parts
    rows = keys_in.shape[1]
    power = jnp.broadcast_to(
        jnp.eye(HEAD_SIZE, dtype=jnp.float32), (rows, HEADS, HEAD_SIZE, HEAD_SIZE)
    )
    carry, unused = lax.scan(
        transition_step, (power, jnp.zeros_like(power)), (keys_in, solved_w, solved_u, kept_masks)
    )
    return carry


def silu_slope(values):
    sigma = jax.nn.sigmoid(values)
    return sigma * (1.0 + values * (1.0 - sigma))


def norm_back(grad_in, values, inverse, gain):
    scaled = grad_in * gain
    return inverse * scaled - values * inverse**3 * jnp.mean(
        scaled * values, axis=-1, keepdims=True
    )


def layer_forward(hidden, weights, head_g, taps, kept_masks):
    mixer_g, mix_w, conv_w, beta_w, out_w, mlp_g, upgate_w, down_w = weights
    rows, block = (hidden.shape[0], hidden.shape[1])
    inverse = lax.rsqrt(jnp.mean(hidden * hidden, axis=-1, keepdims=True) + small_block)
    normed = (hidden * inverse * mixer_g.astype(jnp.float32)).astype(jnp.bfloat16)
    project = jnp.einsum("rtd,de->rte", normed, mix_w, preferred_element_type=jnp.float32)
    betas = jax.nn.sigmoid(
        jnp.einsum("rtd,dh->rth", normed, beta_w, preferred_element_type=jnp.float32)
    )
    before = project[..., : 3 * MODEL_WIDTH]
    gates = project[..., 3 * MODEL_WIDTH :]
    tail = from_behind(before[:, block - (KW - 1) :, :], "seq", 1)
    padded = jnp.concatenate([tail, before], axis=1)
    raw = convolve(padded, conv_w.astype(jnp.float32), taps, block)
    active = jax.nn.silu(raw)
    parts = make_parts(active, betas)
    power, offset_s = transition(parts, kept_masks)
    prefix = forward_doubling((power, offset_s))
    state_in = prefix[1]
    outputs, unused = apply_parts(parts, state_in, kept_masks)
    heads = outputs.reshape(rows, block, HEADS, HEAD_SIZE)
    head_inv = lax.rsqrt(jnp.mean(heads * heads, axis=-1, keepdims=True) + small_head)
    gaussian_sample = heads * head_inv
    head_f = head_g.astype(jnp.float32)
    gated = (
        (gaussian_sample * head_f).reshape(rows, block, MODEL_WIDTH) * jax.nn.silu(gates)
    ).astype(jnp.bfloat16)
    hidden_mid = hidden + jnp.einsum(
        "rtd,de->rte", gated, out_w, preferred_element_type=jnp.float32
    )
    inverse_mid = lax.rsqrt(jnp.mean(hidden_mid * hidden_mid, axis=-1, keepdims=True) + small_block)
    normed_mid = (hidden_mid * inverse_mid * mlp_g.astype(jnp.float32)).astype(jnp.bfloat16)
    upgate = jnp.einsum("rtd,de->rte", normed_mid, upgate_w, preferred_element_type=jnp.float32)
    acted = (jax.nn.silu(upgate[..., :FF]) * upgate[..., FF:]).astype(jnp.bfloat16)
    result = hidden_mid + jnp.einsum(
        "rtf,fd->rtd", acted, down_w, preferred_element_type=jnp.float32
    )
    saved = (
        hidden,
        inverse,
        normed,
        betas,
        gates,
        padded,
        raw,
        active,
        state_in,
        power,
        heads,
        head_inv,
        gaussian_sample,
        gated,
        hidden_mid,
        inverse_mid,
        normed_mid,
        upgate,
        acted,
    )
    return (result, saved)


def layer_backward(grad, saved, weights, head_g, taps, kept_masks):
    (
        hidden,
        inverse,
        normed,
        betas,
        gates,
        padded,
        raw,
        active,
        state_in,
        power,
        heads,
        head_inv,
        gaussian_sample,
        gated,
        hidden_mid,
        inverse_mid,
        normed_mid,
        upgate,
        acted,
    ) = saved
    mixer_g, mix_w, conv_w, beta_w, out_w, mlp_g, upgate_w, down_w = weights
    rows, block = (hidden.shape[0], hidden.shape[1])
    down_grad = grad.astype(jnp.bfloat16)
    grad_down_w = jnp.einsum("rtf,rtd->fd", acted, down_grad, preferred_element_type=jnp.float32)
    grad_acted = jnp.einsum("rtd,fd->rtf", down_grad, down_w, preferred_element_type=jnp.float32)
    gate_part = upgate[..., :FF]
    up_part = upgate[..., FF:]
    grad_upgate = jnp.concatenate(
        [grad_acted * up_part * silu_slope(gate_part), grad_acted * jax.nn.silu(gate_part)], axis=-1
    ).astype(jnp.bfloat16)
    grad_upgate_w = jnp.einsum(
        "rtd,rte->de", normed_mid, grad_upgate, preferred_element_type=jnp.float32
    )
    grad_normed_mid = jnp.einsum(
        "rte,de->rtd", grad_upgate, upgate_w, preferred_element_type=jnp.float32
    )
    grad_mlp_g = jnp.sum(grad_normed_mid * hidden_mid * inverse_mid, axis=(0, 1))
    grad_mid = grad + norm_back(grad_normed_mid, hidden_mid, inverse_mid, mlp_g.astype(jnp.float32))
    attn_grad = grad_mid.astype(jnp.bfloat16)
    grad_out_w = jnp.einsum("rtd,rte->de", gated, attn_grad, preferred_element_type=jnp.float32)
    grad_gated = jnp.einsum("rte,de->rtd", attn_grad, out_w, preferred_element_type=jnp.float32)
    head_f = head_g.astype(jnp.float32)
    grad_gates = (
        grad_gated
        * (gaussian_sample * head_f).reshape(rows, block, MODEL_WIDTH)
        * silu_slope(gates)
    )
    grad_scaled = (grad_gated * jax.nn.silu(gates)).reshape(rows, block, HEADS, HEAD_SIZE)
    grad_head_g = jnp.sum(grad_scaled * gaussian_sample, axis=(0, 1, 2))
    grad_outputs = norm_back(grad_scaled, heads, head_inv, head_f).reshape(rows, block, MODEL_WIDTH)

    def mixer_map(active_in, betas_in, state_start):
        return apply_parts(make_parts(active_in, betas_in), state_start, kept_masks)

    unused, pullback = jax.vjp(mixer_map, active, betas, state_in)
    grad_active, grad_betas, local_term = pullback((grad_outputs, jnp.zeros_like(state_in)))
    flipped = jnp.swapaxes(power, -1, -2)
    suffix = backward_doubling((flipped, local_term))
    more_active, more_betas, ignored = pullback((jnp.zeros_like(grad_outputs), suffix[1]))
    grad_active = grad_active + more_active
    grad_betas = grad_betas + more_betas
    grad_raw = grad_active * silu_slope(raw)

    def conv_map(pad_in, weight_in):
        return convolve(pad_in, weight_in, taps, block)

    unused_conv, conv_pull = jax.vjp(conv_map, padded, conv_w.astype(jnp.float32))
    grad_padded, grad_conv_w = conv_pull(grad_raw)
    returned = from_behind(grad_padded[:, : KW - 1, :].astype(jnp.bfloat16), "seq", -1).astype(
        jnp.float32
    )
    grad_before = grad_padded[:, KW - 1 :, :].at[:, block - (KW - 1) :, :].add(returned)
    grad_project = jnp.concatenate([grad_before, grad_gates], axis=-1).astype(jnp.bfloat16)
    grad_logits = (grad_betas * betas * (1.0 - betas)).astype(jnp.bfloat16)
    grad_mix_w = jnp.einsum("rtd,rte->de", normed, grad_project, preferred_element_type=jnp.float32)
    grad_beta_w = jnp.einsum("rtd,rth->dh", normed, grad_logits, preferred_element_type=jnp.float32)
    grad_normed = jnp.einsum("rte,de->rtd", grad_project, mix_w, preferred_element_type=jnp.float32)
    grad_normed = grad_normed + jnp.einsum(
        "rth,dh->rtd", grad_logits, beta_w, preferred_element_type=jnp.float32
    )
    grad_mixer_g = jnp.sum(grad_normed * hidden * inverse, axis=(0, 1))
    grad_hidden = grad_mid + norm_back(grad_normed, hidden, inverse, mixer_g.astype(jnp.float32))
    terms = (
        grad_mixer_g,
        grad_mix_w,
        grad_conv_w,
        grad_beta_w,
        grad_out_w,
        grad_mlp_g,
        grad_upgate_w,
        grad_down_w,
    )
    return (grad_hidden, terms, grad_head_g)


def shards(
    tokens,
    cotangent,
    starts,
    mixer_gain,
    mix_weight,
    conv_weight,
    beta_weight,
    head_gain,
    out_weight,
    mlp_gain,
    upgate_weight,
    down_weight,
):
    block = tokens.shape[1]
    offset = lax.axis_index("seq") * block
    token_places = offset + jnp.arange(block, dtype=jnp.int32)
    taps = make_taps(starts, token_places)
    kept_masks = build_kept_masks(
        starts, offset + jnp.arange(block // BLOCK_TOKENS, dtype=jnp.int32) * BLOCK_TOKENS
    ).T
    hidden = tokens.astype(jnp.float32)
    kept_weights = []
    layer_index = 0
    weights = (
        lax.all_gather(mixer_gain[layer_index], ("dp", "seq"), axis=0, tiled=True),
        lax.all_gather(mix_weight[layer_index], ("dp", "seq"), axis=0, tiled=True),
        lax.all_gather(conv_weight[layer_index], ("dp", "seq"), axis=1, tiled=True),
        lax.all_gather(beta_weight[layer_index], ("dp", "seq"), axis=0, tiled=True),
        lax.all_gather(out_weight[layer_index], ("dp", "seq"), axis=0, tiled=True),
        lax.all_gather(mlp_gain[layer_index], ("dp", "seq"), axis=0, tiled=True),
        lax.all_gather(upgate_weight[layer_index], ("dp", "seq"), axis=0, tiled=True),
        lax.all_gather(down_weight[layer_index], ("dp", "seq"), axis=0, tiled=True),
    )
    hidden, saved = layer_forward(hidden, weights, head_gain[layer_index], taps, kept_masks)
    kept_weights.append(weights)
    kept_saved = [saved]
    output = hidden.astype(jnp.bfloat16)
    grad = cotangent.astype(jnp.float32)
    big_sums = [None] * LAYERS
    small_terms = [None] * LAYERS
    for layer_index in reversed(range(LAYERS)):
        weights = (
            lax.all_gather(mixer_gain[layer_index], ("dp", "seq"), axis=0, tiled=True),
            lax.all_gather(mix_weight[layer_index], ("dp", "seq"), axis=0, tiled=True),
            lax.all_gather(conv_weight[layer_index], ("dp", "seq"), axis=1, tiled=True),
            lax.all_gather(beta_weight[layer_index], ("dp", "seq"), axis=0, tiled=True),
            lax.all_gather(out_weight[layer_index], ("dp", "seq"), axis=0, tiled=True),
            lax.all_gather(mlp_gain[layer_index], ("dp", "seq"), axis=0, tiled=True),
            lax.all_gather(upgate_weight[layer_index], ("dp", "seq"), axis=0, tiled=True),
            lax.all_gather(down_weight[layer_index], ("dp", "seq"), axis=0, tiled=True),
        )
        grad, terms, head_term = layer_backward(
            grad, kept_saved[layer_index], weights, head_gain[layer_index], taps, kept_masks
        )
        big_sums[layer_index] = (
            lax.psum_scatter(terms[1], ("dp", "seq"), scatter_dimension=0, tiled=True),
            lax.psum_scatter(terms[4], ("dp", "seq"), scatter_dimension=0, tiled=True),
            lax.psum_scatter(terms[6], ("dp", "seq"), scatter_dimension=0, tiled=True),
            lax.psum_scatter(terms[7], ("dp", "seq"), scatter_dimension=0, tiled=True),
        )
        small_terms[layer_index] = (terms[0], terms[2], terms[3], terms[5], head_term)
    big_stack = tuple((jnp.stack([big_sums[0][member]]) for member in range(4)))
    small_stack = tuple((jnp.stack([small_terms[0][member]]) for member in range(5)))
    small_sum = lax.psum(
        (small_stack[0], small_stack[1], small_stack[2], small_stack[3], small_stack[4]),
        ("dp", "seq"),
    )
    total = lax.axis_size(("dp", "seq"))
    place = lax.axis_index(("dp", "seq"))
    width_share = MODEL_WIDTH // total
    conv_share = 3 * MODEL_WIDTH // total
    mixer_part = lax.dynamic_slice_in_dim(small_sum[0], place * width_share, width_share, 1)
    conv_part = lax.dynamic_slice_in_dim(small_sum[1], place * conv_share, conv_share, 2)
    beta_part = lax.dynamic_slice_in_dim(small_sum[2], place * width_share, width_share, 1)
    mlp_part = lax.dynamic_slice_in_dim(small_sum[3], place * width_share, width_share, 1)
    return (
        output,
        grad,
        mixer_part,
        big_stack[0],
        conv_part,
        beta_part,
        small_sum[4],
        big_stack[1],
        mlp_part,
        big_stack[2],
        big_stack[3],
    )


def solution(mesh):
    in_specs = (
        P("dp", "seq", None),
        P("dp", "seq", None),
        P("dp", None),
        P(None, ("dp", "seq")),
        P(None, ("dp", "seq"), None),
        P(None, None, ("dp", "seq")),
        P(None, ("dp", "seq"), None),
        P(),
        P(None, ("dp", "seq"), None),
        P(None, ("dp", "seq")),
        P(None, ("dp", "seq"), None),
        P(None, ("dp", "seq"), None),
    )
    out_specs = (
        P("dp", "seq", None),
        P("dp", "seq", None),
        P(None, ("dp", "seq")),
        P(None, ("dp", "seq"), None),
        P(None, None, ("dp", "seq")),
        P(None, ("dp", "seq"), None),
        P(),
        P(None, ("dp", "seq"), None),
        P(None, ("dp", "seq")),
        P(None, ("dp", "seq"), None),
        P(None, ("dp", "seq"), None),
    )
    return jax.shard_map(shards, mesh=mesh, in_specs=in_specs, out_specs=out_specs, check_vma=False)
```

profile of v0, /device:TPU:0, one launch (start us, length us, event | category | flops | bytes accessed | tf_op | source)
XLA Modules:
  0.0 1869.8 jit_solution(15105247527404711421)
XLA Ops:
  11.2 42.7 %all-reduce.18 = (bf16[1024]{0:T(1024)(128)(2,1)S(1)}, bf16[1024]{0:T(1024)(128)(2,1)S(1)}) all-reduce(bf16[1024]{0:T(1024)(128)(2,1)S(1)} %dynamic-update-slice.3, bf16[1024]{0:T(1024)(128)(2,1)S(1)} %dynamic-update-slice.4), channel_id=3, replica_groups=mesh['dp'=4,'seq'=8] {'dp','seq'}, use_global_device_ids=true, to_apply=%add.15 | all-reduce | flops 2048 | bytes 8192
  56.3 57.3 %all-gather = bf16[1,4,3072]{1,0,2:T(2,128)(2,1)S(1)} all-gather(bf16[1,4,96]{1,0,2:T(2,128)(2,1)S(1)} %copy.298), channel_id=2, replica_groups=mesh['dp'=4,'seq'=8] {'dp','seq'}, dimensions={2}, use_global_device_ids=true | all-gather | bytes 25344 | tf_op jit(solution)/shard_map/all_gather | solution.py:398
  115.4 39.4 %all-gather.3 = bf16[1,1024,8]{2,0,1:T(2,128)(2,1)S(1)} all-gather(bf16[1,32,8]{2,0,1:T(2,128)(2,1)S(1)} %copy.302), channel_id=5, replica_groups=mesh['dp'=4,'seq'=8] {'dp','seq'}, dimensions={1}, use_global_device_ids=true | all-gather | bytes 16896 | tf_op jit(solution)/shard_map/all_gather | solution.py:399
  156.7 63.9 %slice_reduce_fusion.3 = (f32[3072]{0:T(1024)S(1)}, f32[3072]{0:T(1024)S(1)}, f32[3072]{0:T(1024)S(1)}, f32[3072]{0:T(1024)S(1)}) fusion(f32[1,4,3072]{1,0,2:T(1,128)S(1)} %convert_element_type.192), kind=kLoop, calls=%fused_computation.238 | loop fusion | bytes 98304 | tf_op jit(solution)/shard_map/slice | solution.py:52
  245.3 157.3 %custom-call.14 = f32[2,2,8,1,64,64]{4,5,3,2,1,0:T(8,128)S(1)} custom-call(f32[2,2,8,1,64,64]{5,4,3,2,1,0:T(8,128)S(1)} %fusion.187), custom_call_target="InvertDiagBlocksLowerTriangular" | custom-call | tf_op jit(solution)/shard_map/jit(_solve_triangular)/vmap(vmap(vmap()))/triangular_solve/custom-call.1 | solution.py:81
  409.8 17.4 while.94
  444.2 13.7 collective-permute-start.2
  475.8 20.3 %collective-permute-start.3 = (bf16[2,2,8,128,128]{3,4,2,1,0:T(8,128)(2,1)}, bf16[2,2,8,128,128]{3,4,2,1,0:T(8,128)(2,1)}, u32[]{:S(2)}, u32[]{:S(2)}) collective-permute-start(bf16[2,2,8,128,128]{3,4,2,1,0:T(8,128)(2,1)} %pad_maximum_fusion.8), channel_id=1, source_target_pairs={{0,2},{1,3},{2,4},{3,5},{4,6},{5,7},{8,10},{9,11},{10,12},{11,13},... | collective-permute-start | bytes 3145736 | tf_op jit(solution)/shard_map/ppermute | solution.py:23
  496.0 36.7 %collective-permute-done.3 = bf16[2,2,8,128,128]{3,4,2,1,0:T(8,128)(2,1)} collective-permute-done((bf16[2,2,8,128,128]{3,4,2,1,0:T(8,128)(2,1)}, bf16[2,2,8,128,128]{3,4,2,1,0:T(8,128)(2,1)}, u32[]{:S(2)}, u32[]{:S(2)}) %collective-permute-start.3) | collective-permute-done | bytes 1048608 | tf_op jit(solution)/shard_map/ppermute | solution.py:23
  563.9 10.9 collective-permute-done.4
  583.4 14.6 while.91
  613.5 12.8 while.92
  626.3 10.3 fusion.141
  666.3 34.6 %while.95 = (s32[]{:T(128)}, f32[2,8,128,128]{3,2,1,0:T(8,128)S(1)}, f32[2,2,8,64,128]{4,3,2,1,0:T(8,128)}, f32[2,2,8,64,128]{4,3,2,1,0:T(8,128)}, f32[2,2,8,64,...) while((s32[]{:T(128)}, ...), condition=%wide.region_19.21_spmd.clone, body=%wide.region_18.20_spmd.clone.sunk | while | flops 1411252224 | bytes 67119648 | solution.py:179
  711.4 35.6 %collective-permute-done.6 = bf16[2,2,8,128,128]{4,3,2,1,0:T(8,128)(2,1)S(1)} collective-permute-done((bf16[2,2,8,128,128]{4,3,2,1,0:T(8,128)(2,1)S(1)}, bf16[2,2,8,128,128]{4,3,2,1,0:T(8,128)(2,1)S(1)}, u32[]{:S(2)}, u32[]{:S(2)}) %collective-permute-start.6) | collective-permute-done | bytes 1048608 | tf_op jit(solution)/shard_map/ppermute | solution.py:23
  758.6 31.6 %collective-permute-done.7 = bf16[2,2,8,128,128]{4,3,2,1,0:T(8,128)(2,1)} collective-permute-done((bf16[2,2,8,128,128]{4,3,2,1,0:T(8,128)(2,1)}, bf16[2,2,8,128,128]{4,3,2,1,0:T(8,128)(2,1)}, u32[]{:S(2)}, u32[]{:S(2)}) %collective-permute-start.7) | collective-permute-done | bytes 1048608 | tf_op jit(solution)/shard_map/ppermute | solution.py:23
  812.6 35.0 %collective-permute-done.8 = bf16[2,2,8,128,128]{4,3,2,1,0:T(8,128)(2,1)} collective-permute-done((bf16[2,2,8,128,128]{4,3,2,1,0:T(8,128)(2,1)}, bf16[2,2,8,128,128]{4,3,2,1,0:T(8,128)(2,1)}, u32[]{:S(2)}, u32[]{:S(2)}) %collective-permute-start.8) | collective-permute-done | bytes 1048608 | tf_op jit(solution)/shard_map/ppermute | solution.py:23
  855.5 34.2 %while.93 = (s32[]{:T(128)}, f32[2,8,128,128]{3,2,1,0:T(8,128)S(1)}, f32[2,2,8,64,128]{4,3,2,1,0:T(8,128)}, f32[2,2,8,64,128]{4,3,2,1,0:T(8,128)}, f32[2,2,8,64,...) while((s32[]{:T(128)}, ...), condition=%wide.region_23.26_spmd, body=%wide.region_22.25_spmd.sunk | while | flops 1410465792 | bytes 60823540 | solution.py:179
  1013.4 11.2 convolution_bitcast_fusion.8
  1031.6 83.5 %all-reduce.21.cloned.1.call-done = (f32[1,1024]{1,0:T(1,128)}, f32[1,4,3072]{2,1,0:T(4,128)}, f32[1,1024,8]{1,2,0:T(8,128)}, f32[1,128]{1,0:T(1,128)}, f32[1,1024]{1,0:T(1,128)}) async-done(((f32[1,1024]{1,0:T(1,128)}, f32[1,4,3072]{2,1,0:T(4,128)}, f32[1,1024,8]{1,2,0:T(8,128)}, f32[1,128]{1,0:T(1,128)}, f32[1,1024]{1,0:T(1,128)}), (f32[1,1024]{1,0:T(1,128)}, f32[1,4,3072]{2,1,0:T(4,128)}, ...) | async-done | bytes 90640 | tf_op jit(solution)/shard_map/psum | solution.py:435
  1120.1 141.6 %reduce-scatter.7.cloned.1.call-done = f32[32,1024]{1,0:T(8,128)} async-done(((f32[1024,1024]{1,0:T(8,128)}), f32[32,1024]{1,0:T(8,128)}) %reduce-scatter.7.cloned.1.call-update) | async-done | bytes 131088 | tf_op jit(solution)/shard_map/reduce_scatter | solution.py:428
  1261.7 160.0 %reduce-scatter.11.cloned.1.call-done = f32[88,1024]{1,0:T(8,128)} async-done(((f32[2816,1024]{1,0:T(8,128)}), f32[88,1024]{1,0:T(8,128)}) %reduce-scatter.11.cloned.1.call-update) | async-done | bytes 360464 | tf_op jit(solution)/shard_map/reduce_scatter | solution.py:430
  1421.7 187.5 %reduce-scatter.5.cloned.1.call-done = f32[32,4096]{1,0:T(8,128)} async-done(((f32[1024,4096]{1,0:T(8,128)}), f32[32,4096]{1,0:T(8,128)}) %reduce-scatter.5.cloned.1.call-update) | async-done | bytes 524304 | tf_op jit(solution)/shard_map/reduce_scatter | solution.py:427
  1609.2 252.7 %reduce-scatter.9.cloned.1.call-done = f32[32,5632]{1,0:T(8,128)} async-done(((f32[1024,5632]{1,0:T(8,128)}), f32[32,5632]{1,0:T(8,128)}) %reduce-scatter.9.cloned.1.call-update) | async-done | bytes 720912 | tf_op jit(solution)/shard_map/reduce_scatter | solution.py:429
  (658 shorter events, 459.6 us)
Async XLA Ops:
  7.2 108.2 %copy-start.144 = (bf16[1,32,8]{1,2,0:T(8,128)(2,1)S(1)}, bf16[1,32,8]{1,2,0:T(8,128)(2,1)}, u32[]{:S(2)}) copy-start(bf16[1,32,8]{1,2,0:T(8,128)(2,1)} %param.36) | copy-start | bytes 1540
  7.2 213.5 %all-gather.13.cloned.1.call-start = ((), (), s32[]{:S(2)}) async-start(), calls=%async_computation.8 | async-start | bytes 8650752 | tf_op jit(solution)/shard_map/all_gather | solution.py:397
  7.9 600.9 %all-gather.15.cloned.1.call-start = ((), (), s32[]{:S(2)}) async-start(), calls=%async_computation.9 | async-start | bytes 2162688 | tf_op jit(solution)/shard_map/all_gather | solution.py:400
  8.7 146.4 %copy-start.31 = (bf16[2,128,1024]{2,1,0:T(8,128)(2,1)S(1)}, bf16[2,128,1024]{2,1,0:T(8,128)(2,1)}, u32[]{:S(2)}) copy-start(bf16[2,128,1024]{2,1,0:T(8,128)(2,1)} %param.30) | copy-start | bytes 1572868
  8.7 617.6 %all-gather.17.cloned.1.call-start = ((), (), s32[]{:S(2)}) async-start(), calls=%async_computation.10 | async-start | bytes 11894784 | tf_op jit(solution)/shard_map/all_gather | solution.py:402
  9.4 627.2 %all-gather.19.cloned.1.call-start = ((), (), s32[]{:S(2)}) async-start(), calls=%async_computation.11 | async-start | bytes 5947392 | tf_op jit(solution)/shard_map/all_gather | solution.py:403
  53.9 166.8 %copy-start.104 = (f32[1024]{0:T(1024)}, f32[1024]{0:T(1024)S(1)}, u32[]{:S(2)}) copy-start(f32[1024]{0:T(1024)S(1)} %convert_element_type.195) | copy-start | bytes 12292
  156.3 250.2 %copy-start.100 = (f32[2,2,64,8]{2,3,0,1:T(8,128)}, f32[2,2,64,8]{2,3,0,1:T(8,128)S(1)}, u32[]{:S(2)}) copy-start(f32[2,2,64,8]{2,3,0,1:T(8,128)S(1)} %copy.443) | copy-start | bytes 24580
  226.6 3.1 collective-permute-start
  431.7 8.1 collective-permute-start.1
  444.2 16.2 collective-permute-start.2
  458.0 657.0 %all-reduce.21.cloned.1.call-start = ((), (), s32[]{:S(2)}) async-start(), calls=%async_computation.12 | async-start | bytes 181248 | tf_op jit(solution)/shard_map/psum | solution.py:435
  462.4 112.4 %copy-start.15 = (f32[1,2,8,128,128]{4,3,2,1,0:T(8,128)}, f32[1,2,8,128,128]{4,3,2,1,0:T(8,128)S(1)}, u32[]{:S(2)}) copy-start(f32[1,2,8,128,128]{4,3,2,1,0:T(8,128)S(1)} %stack_broadcast_in_dim.4) | copy-start | bytes 3145732
  475.8 57.0 %collective-permute-start.3 = (bf16[2,2,8,128,128]{3,4,2,1,0:T(8,128)(2,1)}, bf16[2,2,8,128,128]{3,4,2,1,0:T(8,128)(2,1)}, u32[]{:S(2)}, u32[]{:S(2)}) collective-permute-start(bf16[2,2,8,128,128]{3,4,2,1,0:T(8,128)(2,1)} %pad_maximum_fusion.8), channel_id=1, source_target_pairs={{0,2},{1,3},{2,4},{3,5},{4,6},{5,7},{8,10},{9,11},{10,12},{11,13},... | collective-permute-start | bytes 3145736 | tf_op jit(solution)/shard_map/ppermute | solution.py:23
  547.8 27.0 %collective-permute-start.4 = (bf16[2,2,8,128,128]{3,4,2,1,0:T(8,128)(2,1)}, bf16[2,2,8,128,128]{3,4,2,1,0:T(8,128)(2,1)}, u32[]{:S(2)}, u32[]{:S(2)}) collective-permute-start(bf16[2,2,8,128,128]{3,4,2,1,0:T(8,128)(2,1)} %pad_maximum_fusion.9), channel_id=1, source_target_pairs={{0,4},{1,5},{2,6},{3,7},{8,12},{9,13},{10,14},{11,15},{16,20},{17,... | collective-permute-start | bytes 3145736 | tf_op jit(solution)/shard_map/ppermute | solution.py:23
  703.2 4.9 collective-permute-start.5
  709.9 37.1 %collective-permute-start.6 = (bf16[2,2,8,128,128]{4,3,2,1,0:T(8,128)(2,1)S(1)}, bf16[2,2,8,128,128]{4,3,2,1,0:T(8,128)(2,1)S(1)}, u32[]{:S(2)}, u32[]{:S(2)}) collective-permute-start(bf16[2,2,8,128,128]{4,3,2,1,0:T(8,128)(2,1)S(1)} %fusion.257), channel_id=1, source_target_pairs={{1,0},{2,1},{3,2},{4,3},{5,4},{6,5},{7,6},{9,8},{10,9},{11,10},{12... | collective-permute-start | bytes 3145736 | tf_op jit(solution)/shard_map/ppermute | solution.py:23
  753.5 36.6 %collective-permute-start.7 = (bf16[2,2,8,128,128]{4,3,2,1,0:T(8,128)(2,1)}, bf16[2,2,8,128,128]{4,3,2,1,0:T(8,128)(2,1)}, u32[]{:S(2)}, u32[]{:S(2)}) collective-permute-start(bf16[2,2,8,128,128]{4,3,2,1,0:T(8,128)(2,1)} %pad_maximum_fusion.11), channel_id=1, source_target_pairs={{2,0},{3,1},{4,2},{5,3},{6,4},{7,5},{10,8},{11,9},{12,10},{13,11},... | collective-permute-start | bytes 3145736 | tf_op jit(solution)/shard_map/ppermute | solution.py:23
  796.3 51.4 %collective-permute-start.8 = (bf16[2,2,8,128,128]{4,3,2,1,0:T(8,128)(2,1)}, bf16[2,2,8,128,128]{4,3,2,1,0:T(8,128)(2,1)}, u32[]{:S(2)}, u32[]{:S(2)}) collective-permute-start(bf16[2,2,8,128,128]{4,3,2,1,0:T(8,128)(2,1)} %pad_maximum_fusion.12), channel_id=1, source_target_pairs={{4,0},{5,1},{6,2},{7,3},{12,8},{13,9},{14,10},{15,11},{20,16},{21,... | collective-permute-start | bytes 3145736 | tf_op jit(solution)/shard_map/ppermute | solution.py:23
  976.7 5.4 collective-permute-start.9
  991.3 270.5 %reduce-scatter.7.cloned.1.call-start = ((), (), s32[]{:S(2)}) async-start(), calls=%async_computation.5 | async-start | bytes 4325376 | tf_op jit(solution)/shard_map/reduce_scatter | solution.py:428
  995.1 426.6 %reduce-scatter.11.cloned.1.call-start = ((), (), s32[]{:S(2)}) async-start(), calls=%async_computation.7 | async-start | bytes 11894784 | tf_op jit(solution)/shard_map/reduce_scatter | solution.py:430
  1002.6 606.6 %reduce-scatter.5.cloned.1.call-start = ((), (), s32[]{:S(2)}) async-start(), calls=%async_computation.4 | async-start | bytes 17301504 | tf_op jit(solution)/shard_map/reduce_scatter | solution.py:427
  1012.1 849.7 %reduce-scatter.9.cloned.1.call-start = ((), (), s32[]{:S(2)}) async-start(), calls=%async_computation.6 | async-start | bytes 23789568 | tf_op jit(solution)/shard_map/reduce_scatter | solution.py:429
  (169 other events, 1631.7 us)
Sparse Core Ops, SparseCore 0:
  11.0 87.5 all-gather.12
  101.6 56.2 all-gather.14
  160.8 90.6 all-gather.16
  458.1 76.4 all-gather.18
  991.4 123.5 all-reduce.20
  1117.7 143.9 reduce-scatter.6
  1264.6 157.0 reduce-scatter.10
  1424.6 184.5 reduce-scatter.4
  1612.1 249.7 reduce-scatter.8
where the time goes:
time: 1880 us; the launch traced here: 1870 us
  waiting for transfers between devices  985 us (52%)
  matrix products  267 us (14%)
  other arithmetic  221 us (12%)
  local copies, waits for them, and re-layouts  179 us (10%)
  blocking collectives  139 us (7%)
  starting transfers between devices  58.7 us (3%)
    reduce_scatter x1, waiting for transfers between devices, shards(): lax.psum_scatter(terms[6], ('dp', 'seq'), scatter_dimension=0, tiled=True)  253 us
    reduce_scatter x1, waiting for transfers between devices, shards(): lax.psum_scatter(terms[1], ('dp', 'seq'), scatter_dimension=0, tiled=True)  187 us
    reduce_scatter x1, waiting for transfers between devices, shards(): lax.psum_scatter(terms[7], ('dp', 'seq'), scatter_dimension=0, tiled=True)  160 us
    another operation x5, other arithmetic, block_parts(): jax.scipy.linalg.solve_triangular(system, weighted * keys_in, lower=True,...  158 us
    ppermute x10, waiting for transfers between devices, from_behind(): lax.ppermute(value, axis, [(source, source + steps) for source in range(i...  158 us
    reduce_scatter x1, waiting for transfers between devices, shards(): lax.psum_scatter(terms[4], ('dp', 'seq'), scatter_dimension=0, tiled=True)  142 us
    psum x1, waiting for transfers between devices, shards(): lax.psum((small_stack[0], small_stack[1], small_stack[2], small_stack[3],...  83.5 us
    slice x1, local copies, waits for them, and re-layouts, convolve(): weight[shift_by] * padded[:, begin:begin + length]  63.9 us
  transfers between devices with their start and end apart: 19, of which 14 were waited for; matrix products, arithmetic and copies ran while one was open for 23% of the time, Pallas kernels for 0%

commit v1 on v0

v1 whole, which is shorter than its diff:
```python
import functools

import jax
import jax.numpy as jnp
from jax import lax
from jax.experimental import pallas as pl
from jax.experimental.pallas import tpu as pltpu
from jax.sharding import PartitionSpec as P

MODEL_WIDTH = 1024
HEADS = 8
HEAD_SIZE = 128
FF = 2816
KW = 4
PACKED = 4

MESH = pl.DeviceIdType.MESH
F32 = jnp.float32
BF16 = jnp.bfloat16
TOKENS = 128
ROWS = 2
ALL = ROWS * TOKENS
HALO = 8
NEAR_ZERO = 1e-06
HEAD_ZERO = 1e-05
MIX = 4 * MODEL_WIDTH
QKV = 3 * MODEL_WIDTH
SMALL = 256
BETA_AT = 2
CONV_AT = 10
AT_SMALL = MIX
AT_OUT = AT_SMALL + SMALL
AT_UP = AT_OUT + MODEL_WIDTH
AT_DOWN = AT_UP + 2 * FF
PACK = AT_DOWN + FF
CHUNK = PACK // 12


def nn(a, b):
    return lax.dot_general(a, b, (((1,), (0,)), ((), ())), preferred_element_type=F32)


def nt(a, b):
    return lax.dot_general(a, b, (((1,), (1,)), ((), ())), preferred_element_type=F32)


def tn(a, b):
    return lax.dot_general(a, b, (((0,), (0,)), ((), ())), preferred_element_type=F32)


def low(value):
    return value.astype(BF16)


def when(condition, action):
    if condition is None:
        action()
    else:
        pl.when(condition)(action)


def segment(starts, row, places):
    total = jnp.zeros_like(places)
    for k in range(PACKED):
        begin = starts[row, k]
        total = total + jnp.where((begin > 0) & (places >= begin), 1, 0)
    return total


def row_scalars(starts, row, first):
    before = jnp.int32(0)
    last = jnp.int32(0)
    for k in range(PACKED):
        begin = starts[row, k]
        before = before + jnp.where((begin > 0) & (begin <= first - 1), 1, 0)
        last = last + jnp.where((begin > 0) & (begin <= first + TOKENS - 1), 1, 0)
    return before, last


def fill_masks(starts, first, carry_in, carry_out, taps, within, below):
    places = first + lax.broadcasted_iota(jnp.int32, (TOKENS, HEAD_SIZE), 0)
    side = lax.broadcasted_iota(jnp.int32, (TOKENS, TOKENS), 0)
    across = lax.broadcasted_iota(jnp.int32, (TOKENS, TOKENS), 1)
    within[...] = jnp.zeros_like(within)
    below[...] = jnp.zeros_like(below)
    for row in range(ROWS):
        span = pl.ds(row * TOKENS, TOKENS)
        mine = segment(starts, row, places)
        before, last = row_scalars(starts, row, first)
        carry_in[span, :] = (mine == before).astype(F32)
        carry_out[span, :] = (mine == last).astype(F32)
        for shift in range(1, KW):
            there = places - shift
            same = (segment(starts, row, there) == mine) & (there >= 0)
            taps[shift - 1, span, :] = same.astype(F32)
        same = segment(starts, row, first + side) == segment(starts, row, first + across)
        within[span, span] = (same & (side >= across)).astype(F32)
        below[span, span] = (same & (side > across)).astype(F32)


def padded(main, halo):
    return jnp.concatenate([halo, main], axis=0)


def unit_scale(values):
    return lax.rsqrt(jnp.sum(values * values, axis=-1, keepdims=True) + NEAR_ZERO)


def lane_of(values, lane):
    lanes = lax.broadcasted_iota(jnp.int32, values.shape, 1)
    return jnp.sum(jnp.where(lanes == lane, values, 0.0), axis=-1, keepdims=True)


def head_columns(part, head):
    return pl.ds(pl.multiple_of(part * MODEL_WIDTH + head * HEAD_SIZE, HEAD_SIZE), HEAD_SIZE)


def halves(value):
    high = low(value)
    return high, low(value - high.astype(F32))


def gram_of(keys):
    high, rest = halves(keys)
    return nt(high, high) + nt(high, rest) + nt(rest, high)


def per_row(function, *arrays):
    return jnp.concatenate(
        [
            function(row, *[array[row * TOKENS : (row + 1) * TOKENS] for array in arrays])
            for row in range(ROWS)
        ],
        axis=0,
    )


def invert(system, apart):
    eye = jnp.where(apart == 0, 1.0, 0.0)
    solved = eye - jnp.where(apart == 1, system, 0.0)
    size = 2
    while size < TOKENS:
        cross = low(jnp.where((apart >= size) & (apart < 2 * size), system, 0.0))
        rough = low(solved)
        solved = solved - nn(low(nn(rough, cross)), rough)
        size *= 2
    return solved


def kappa_eye(kept):
    side = lax.broadcasted_iota(jnp.int32, (HEAD_SIZE, HEAD_SIZE), 0)
    across = lax.broadcasted_iota(jnp.int32, (HEAD_SIZE, HEAD_SIZE), 1)
    return jnp.where(side == across, 1.0, 0.0) * kept


def mixer_forward_kernel(
    starts, tokens, halo, mixer_gain, mix, small, conv, head_gain,
    normed, pre, raw, beta, solved, solved_w, fresh, state, power, outputs, gated,
    every, carry_in, carry_out, taps, within, below, apart,
    offset, solved_u, attend, queries, arriving, leaving, send, receive,
):
    count = lax.axis_size("seq")
    index = lax.axis_index("seq")
    first = index * TOKENS
    barrier = pltpu.get_barrier_semaphore()

    @pl.when(index > 0)
    def _():
        pl.semaphore_signal(barrier, inc=1, device_id={"seq": index - 1}, device_id_type=MESH)

    @pl.when(index == 0)
    def _():
        arriving[...] = jnp.zeros_like(arriving)

    fill_masks(starts, first, carry_in, carry_out, taps, within, below)
    side = lax.broadcasted_iota(jnp.int32, (ALL, ALL), 0)
    across = lax.broadcasted_iota(jnp.int32, (ALL, ALL), 1)
    apart[...] = jnp.bitwise_xor(side, across)

    def norm(source, target, rows):
        values = source[...].astype(F32)
        scale = lax.rsqrt(jnp.mean(values * values, axis=-1, keepdims=True) + NEAR_ZERO)
        target[rows, :] = low(values * scale * mixer_gain[...])

    norm(tokens, every, pl.ds(0, ALL))
    norm(halo, every, pl.ds(ALL, ROWS * HALO))
    normed[...] = every[pl.ds(0, ALL), :]
    beta[...] = jax.nn.sigmoid(nn(every[pl.ds(0, ALL), :], small[...]))

    def project(step, _):
        columns = pl.ds(pl.multiple_of(step * 512, 512), 512)
        pre[:, columns] = nn(every[...], mix[:, columns])
        return 0

    lax.fori_loop(0, MIX // 512, project, 0)

    def convolve(columns):
        weight = conv[:, columns]
        rows = []
        for row in range(ROWS):
            main = pre[pl.ds(row * TOKENS, TOKENS), columns]
            before = pre[pl.ds(ALL + row * HALO, HALO), columns]
            longer = padded(main, before)
            total = weight[0:1] * main
            for shift in range(1, KW):
                tap = taps[shift - 1, pl.ds(row * TOKENS, TOKENS), :]
                total = total + weight[shift : shift + 1] * longer[HALO - shift : HALO - shift + TOKENS] * tap
            rows.append(total)
        total = jnp.concatenate(rows, axis=0)
        raw[:, columns] = total
        return total * jax.nn.sigmoid(total)

    def local(head):
        active_q = convolve(head_columns(0, head))
        active_k = convolve(head_columns(1, head))
        values = convolve(head_columns(2, head))
        query = active_q * (unit_scale(active_q) * HEAD_SIZE**-0.5)
        key = active_k * unit_scale(active_k)
        strength = lane_of(beta[...], BETA_AT + head)
        columns = head_columns(0, head)
        system = below[...] * (strength * gram_of(key))
        inverse = low(invert(system, apart[...]))
        solved[head] = inverse
        enter = carry_in[...]
        w = low(nn(inverse, low(strength * enter * key)))
        u = nn(inverse, low(strength * values))
        solved_w[:, columns] = w
        solved_u[:, columns] = u
        leave = low(carry_out[...] * key)
        u_low = low(u)
        for row in range(ROWS):
            span = slice(row * TOKENS, (row + 1) * TOKENS)
            before, last = row_scalars(starts, row, first)
            kept = jnp.where(before == last, 1.0, 0.0)
            power[head, row] = low(kappa_eye(kept) - tn(leave[span], w[span]))
            offset[head, row] = tn(leave[span], u_low[span])
        attend[head] = low(within[...] * nt(low(query), low(key)))
        queries[:, columns] = low(enter * query)

    def pair(step, _):
        for part in range(GROUP):
            local(step * GROUP + part)
        return 0

    lax.fori_loop(0, HEADS // GROUP, pair, 0)

    @pl.when(index + 1 < count)
    def _():
        pl.semaphore_wait(barrier, 1)

    def copy(head):
        return pltpu.make_async_remote_copy(
            src_ref=leaving.at[head], dst_ref=arriving.at[head], send_sem=send.at[head], recv_sem=receive.at[head],
            device_id={"seq": index + 1}, device_id_type=MESH,
        )

    def chain(head, _):
        @pl.when(index > 0)
        def _():
            copy(head).wait_recv()

        @pl.when(index + 1 < count)
        def _():
            for row in range(ROWS):
                leaving[head, row] = low(nn(power[head, row], arriving[head, row]) + offset[head, row])
            copy(head).start()

        columns = head_columns(0, head)
        w, u, query = solved_w[:, columns], solved_u[:, columns], queries[:, columns]
        x = low(u - per_row(lambda row, part: nn(part, arriving[head, row]), w))
        fresh[:, columns] = x
        output = per_row(lambda row, part: nn(part, arriving[head, row]), query) + nn(attend[head], x)
        outputs[:, columns] = output
        scale = lax.rsqrt(jnp.mean(output * output, axis=-1, keepdims=True) + HEAD_ZERO)
        gate = pre[pl.ds(0, ALL), head_columns(3, head)]
        gated[:, columns] = low(output * scale * head_gain[...] * (gate * jax.nn.sigmoid(gate)))
        return 0

    lax.fori_loop(0, HEADS, chain, 0)
    state[...] = arriving[...]

    @pl.when(index + 1 < count)
    def _():
        def drain(head, _):
            copy(head).wait_send()
            return 0

        lax.fori_loop(0, HEADS, drain, 0)


GROUP = 2


def mixer_forward(starts, tokens, halo, mixer_gain, mix, small, conv, head_gain):
    vmem = pl.BlockSpec(memory_space=pltpu.VMEM)
    shape = jax.ShapeDtypeStruct
    states = (HEADS, ROWS, HEAD_SIZE, HEAD_SIZE)
    return pl.pallas_call(
        mixer_forward_kernel,
        out_shape=[
            shape((ALL, MODEL_WIDTH), BF16),
            shape((ALL + ROWS * HALO, MIX), F32),
            shape((ALL, QKV), F32),
            shape((ALL, SMALL), F32),
            shape((HEADS, ALL, ALL), BF16),
            shape((ALL, MODEL_WIDTH), BF16),
            shape((ALL, MODEL_WIDTH), BF16),
            shape(states, BF16),
            shape(states, BF16),
            shape((ALL, MODEL_WIDTH), F32),
            shape((ALL, MODEL_WIDTH), BF16),
        ],
        in_specs=[pl.BlockSpec(memory_space=pltpu.SMEM)] + [vmem] * 7,
        out_specs=[vmem] * 11,
        scratch_shapes=[
            pltpu.VMEM((ALL + ROWS * HALO, MODEL_WIDTH), BF16),
            pltpu.VMEM((ALL, HEAD_SIZE), F32),
            pltpu.VMEM((ALL, HEAD_SIZE), F32),
            pltpu.VMEM((KW - 1, ALL, HEAD_SIZE), F32),
            pltpu.VMEM((ALL, ALL), F32),
            pltpu.VMEM((ALL, ALL), F32),
            pltpu.VMEM((ALL, ALL), jnp.int32),
            pltpu.VMEM(states, F32),
            pltpu.VMEM((ALL, MODEL_WIDTH), F32),
            pltpu.VMEM((HEADS, ALL, ALL), BF16),
            pltpu.VMEM((ALL, MODEL_WIDTH), BF16),
            pltpu.VMEM(states, BF16),
            pltpu.VMEM(states, BF16),
            pltpu.SemaphoreType.DMA((HEADS,)),
            pltpu.SemaphoreType.DMA((HEADS,)),
        ],
        compiler_params=pltpu.CompilerParams(
            collective_id=3, has_side_effects=True, vmem_limit_bytes=56 * 2**20
        ),
        name="mixer_forward",
    )(starts, tokens, halo, mixer_gain, mix, small, conv, head_gain)


def mixer_backward_kernel(
    starts, grad_gated, grad_mid, tokens, mixer_gain, mix, small, conv, head_gain,
    pre, raw, beta, solved, solved_w, fresh, state, power, outputs,
    grad_hidden, grad_project, grad_logits, grad_conv, grad_head, grad_gain,
    carry_in, carry_out, taps, within, below,
    grad_out, fresh_part, offset, grad_raw, grad_beta, arriving, leaving, halo_out, halo_in,
    send, receive, halo_send, halo_receive,
):
    count = lax.axis_size("seq")
    index = lax.axis_index("seq")
    first = index * TOKENS
    barrier = pltpu.get_barrier_semaphore()

    @pl.when(index + 1 < count)
    def _():
        pl.semaphore_signal(barrier, inc=1, device_id={"seq": index + 1}, device_id_type=MESH)

    @pl.when(index + 1 == count)
    def _():
        arriving[...] = jnp.zeros_like(arriving)
        halo_in[...] = jnp.zeros_like(halo_in)

    fill_masks(starts, first, carry_in, carry_out, taps, within, below)
    grad_head[...] = jnp.zeros_like(grad_head)
    grad_beta[...] = jnp.zeros_like(grad_beta)

    def active_of(part, head):
        values = raw[:, head_columns(part, head)]
        return values * jax.nn.sigmoid(values)

    def prepare(head):
        columns = head_columns(0, head)
        gate_columns = head_columns(3, head)
        gate = pre[pl.ds(0, ALL), gate_columns]
        sigma = jax.nn.sigmoid(gate)
        output = outputs[:, columns]
        scale = lax.rsqrt(jnp.mean(output * output, axis=-1, keepdims=True) + HEAD_ZERO)
        sample = output * scale
        incoming = grad_gated[:, columns]
        gain = head_gain[...]
        grad_project[:, gate_columns] = low(incoming * sample * gain * (sigma * (1.0 + gate * (1.0 - sigma))))
        grad_sample = incoming * (gate * sigma)
        grad_head[0:1, :] += jnp.sum(grad_sample * sample, axis=0, keepdims=True)
        scaled = grad_sample * gain
        mean = jnp.mean(scaled * output, axis=-1, keepdims=True)
        here = low(scale * scaled - output * (scale * scale * scale * mean))
        grad_out[:, columns] = here
        active_q, active_k = active_of(0, head), active_of(1, head)
        query = active_q * (unit_scale(active_q) * HEAD_SIZE**-0.5)
        key = active_k * unit_scale(active_k)
        attend = low(within[...] * nt(low(query), low(key)))
        part = tn(attend, here)
        fresh_part[:, columns] = part
        entering = low(carry_in[...] * query)
        part_low = low(part)
        w = solved_w[:, columns]
        for row in range(ROWS):
            span = slice(row * TOKENS, (row + 1) * TOKENS)
            offset[head, row] = tn(entering[span], here[span]) - tn(w[span], part_low[span])

    def prepare_some(step, _):
        for part in range(GROUP):
            prepare(step * GROUP + part)
        return 0

    lax.fori_loop(0, HEADS // GROUP, prepare_some, 0)

    @pl.when(index > 0)
    def _():
        pl.semaphore_wait(barrier, 1)

    def copy(head):
        return pltpu.make_async_remote_copy(
            src_ref=leaving.at[head], dst_ref=arriving.at[head], send_sem=send.at[head], recv_sem=receive.at[head],
            device_id={"seq": index - 1}, device_id_type=MESH,
        )

    def chain(head, _):
        @pl.when(index + 1 < count)
        def _():
            copy(head).wait_recv()

        @pl.when(index > 0)
        def _():
            for row in range(ROWS):
                leaving[head, row] = low(tn(power[head, row], arriving[head, row]) + offset[head, row])
            copy(head).start()

        return 0

    lax.fori_loop(0, HEADS, chain, 0)

    def finish(head):
        columns = head_columns(0, head)
        raw_q, raw_k = raw[:, columns], raw[:, head_columns(1, head)]
        raw_v = raw[:, head_columns(2, head)]
        sigma_q, sigma_k, sigma_v = jax.nn.sigmoid(raw_q), jax.nn.sigmoid(raw_k), jax.nn.sigmoid(raw_v)
        active_q, active_k, values = raw_q * sigma_q, raw_k * sigma_k, raw_v * sigma_v
        scale_q, scale_k = unit_scale(active_q), unit_scale(active_k)
        query = low(active_q * (scale_q * HEAD_SIZE**-0.5))
        key_full = active_k * scale_k
        key = low(key_full)
        enter, leave = carry_in[...], carry_out[...]
        strength = lane_of(beta[...], BETA_AT + head)
        here = grad_out[:, columns]
        x = fresh[:, columns]
        leaving_keys = low(leave * key_full)
        grad_x = fresh_part[:, columns] + per_row(lambda row, part: nn(part, arriving[head, row]), leaving_keys)
        y = tn(solved[head], low(grad_x))
        y_low = low(y)
        grad_attend = low(within[...] * nt(here, x))
        gram = nt(key, key)
        grad_system = -below[...] * nt(y_low, x)
        grad_gram = low(strength * grad_system)
        grad_q = nn(grad_attend, key) + enter * per_row(lambda row, part: nt(part, state[head, row]), here)
        grad_k = (
            tn(grad_attend, query)
            + leave * per_row(lambda row, part: nt(part, arriving[head, row]), x)
            + nn(grad_gram, key)
            + tn(grad_gram, key)
            - strength * enter * per_row(lambda row, part: nt(part, state[head, row]), y_low)
        )
        z = values - enter * per_row(lambda row, part: nn(part, state[head, row]), key)
        grad_v = strength * y
        grad_strength = jnp.sum(y * z, axis=-1, keepdims=True) + jnp.sum(grad_system * gram, axis=-1, keepdims=True)
        lanes = lax.broadcasted_iota(jnp.int32, grad_beta.shape, 1)
        grad_beta[...] = jnp.where(lanes == BETA_AT + head, grad_strength, grad_beta[...])

        def through(grad, active, scale, part, sigma, extra):
            grad = grad * extra
            mean = jnp.sum(active * grad, axis=-1, keepdims=True)
            grad = scale * grad - active * (scale * scale * scale * mean)
            return grad * (sigma * (1.0 + part * (1.0 - sigma)))

        grad_raw[:, columns] = through(grad_q, active_q, scale_q, raw_q, sigma_q, HEAD_SIZE**-0.5)
        grad_raw[:, head_columns(1, head)] = through(grad_k, active_k, scale_k, raw_k, sigma_k, 1.0)
        grad_raw[:, head_columns(2, head)] = grad_v * (sigma_v * (1.0 + raw_v * (1.0 - sigma_v)))

    def finish_some(step, _):
        for part in range(GROUP):
            finish(step * GROUP + part)
        return 0

    lax.fori_loop(0, HEADS // GROUP, finish_some, 0)

    def convolve_back(step, _):
        columns = pl.ds(pl.multiple_of(step * HEAD_SIZE, HEAD_SIZE), HEAD_SIZE)
        weight = conv[:, columns]
        nothing = jnp.zeros((HALO, HEAD_SIZE), F32)
        sums = [jnp.zeros((1, HEAD_SIZE), F32) for _ in range(KW)]
        early = []
        for row in range(ROWS):
            span = pl.ds(row * TOKENS, TOKENS)
            grad = grad_raw[span, columns]
            main = pre[span, columns]
            longer = padded(main, pre[pl.ds(ALL + row * HALO, HALO), columns])
            total = weight[0:1] * jnp.concatenate([nothing, grad], axis=0)
            sums[0] = sums[0] + jnp.sum(grad * main, axis=0, keepdims=True)
            for shift in range(1, KW):
                masked = grad * taps[shift - 1, span, :]
                wide = jnp.concatenate([nothing, masked, nothing], axis=0)
                total = total + weight[shift : shift + 1] * wide[shift : shift + HALO + TOKENS]
                before = longer[HALO - shift : HALO - shift + TOKENS]
                sums[shift] = sums[shift] + jnp.sum(masked * before, axis=0, keepdims=True)
            early.append(total[:HALO])
            grad_raw[span, columns] = total[HALO:]
        halo_out[:, columns] = low(jnp.concatenate(early, axis=0))
        grad_conv[:, columns] = jnp.concatenate(sums, axis=0)
        return 0

    lax.fori_loop(0, QKV // HEAD_SIZE, convolve_back, 0)
    back = pltpu.make_async_remote_copy(
        src_ref=halo_out, dst_ref=halo_in, send_sem=halo_send, recv_sem=halo_receive,
        device_id={"seq": index - 1}, device_id_type=MESH,
    )

    @pl.when(index > 0)
    def _():
        back.start()

    strengths = beta[...]
    grad_logits[...] = low(grad_beta[...] * strengths * (1.0 - strengths))

    @pl.when(index + 1 < count)
    def _():
        back.wait_recv()

    for row in range(ROWS):
        end = pl.ds((row + 1) * TOKENS - HALO, HALO)
        grad_raw[end, :] += halo_in[...].astype(F32)[row * HALO : (row + 1) * HALO]
    grad_project[:, pl.ds(0, QKV)] = low(grad_raw[...])

    def normed_back(step, _):
        rows = pl.ds(pl.multiple_of(step * 256, 256), 256)
        grad_hidden[:, rows] = nt(grad_project[...], mix[rows, :]) + nt(grad_logits[...], small[rows, :])
        return 0

    lax.fori_loop(0, MODEL_WIDTH // 256, normed_back, 0)
    hidden = tokens[...].astype(F32)
    scale = lax.rsqrt(jnp.mean(hidden * hidden, axis=-1, keepdims=True) + NEAR_ZERO)
    grad = grad_hidden[...]
    grad_gain[...] = jnp.sum(grad * hidden * scale, axis=0, keepdims=True)
    scaled = grad * mixer_gain[...]
    mean = jnp.mean(scaled * hidden, axis=-1, keepdims=True)
    grad_hidden[...] = grad_mid[...] + scale * scaled - hidden * (scale * scale * scale * mean)

    @pl.when(index > 0)
    def _():
        back.wait_send()

        def drain(head, _):
            copy(head).wait_send()
            return 0

        lax.fori_loop(0, HEADS, drain, 0)


def mixer_backward(*operands):
    vmem = pl.BlockSpec(memory_space=pltpu.VMEM)
    shape = jax.ShapeDtypeStruct
    states = (HEADS, ROWS, HEAD_SIZE, HEAD_SIZE)
    return pl.pallas_call(
        mixer_backward_kernel,
        out_shape=[
            shape((ALL, MODEL_WIDTH), F32),
            shape((ALL, MIX), BF16),
            shape((ALL, SMALL), BF16),
            shape((KW, QKV), F32),
            shape((8, HEAD_SIZE), F32),
            shape((1, MODEL_WIDTH), F32),
        ],
        in_specs=[pl.BlockSpec(memory_space=pltpu.SMEM)] + [vmem] * 17,
        out_specs=[vmem] * 6,
        scratch_shapes=[
            pltpu.VMEM((ALL, HEAD_SIZE), F32),
            pltpu.VMEM((ALL, HEAD_SIZE), F32),
            pltpu.VMEM((KW - 1, ALL, HEAD_SIZE), F32),
            pltpu.VMEM((ALL, ALL), F32),
            pltpu.VMEM((ALL, ALL), F32),
            pltpu.VMEM((ALL, MODEL_WIDTH), BF16),
            pltpu.VMEM((ALL, MODEL_WIDTH), F32),
            pltpu.VMEM(states, F32),
            pltpu.VMEM((ALL, QKV), F32),
            pltpu.VMEM((ALL, SMALL), F32),
            pltpu.VMEM(states, BF16),
            pltpu.VMEM(states, BF16),
            pltpu.VMEM((ROWS * HALO, QKV), BF16),
            pltpu.VMEM((ROWS * HALO, QKV), BF16),
            pltpu.SemaphoreType.DMA((HEADS,)),
            pltpu.SemaphoreType.DMA((HEADS,)),
            pltpu.SemaphoreType.DMA,
            pltpu.SemaphoreType.DMA,
        ],
        compiler_params=pltpu.CompilerParams(
            collective_id=4, has_side_effects=True, vmem_limit_bytes=56 * 2**20
        ),
        name="mixer_backward",
    )(*operands)


def place():
    row, spot = lax.axis_index("dp"), lax.axis_index("seq")
    level, core = spot // 2, lax.rem(spot, 2)
    near = row + 1 - 2 * lax.rem(row, 2)
    far = row + 2 - 4 * (row // 2)
    first = near * (1 - core) + far * core
    second = far * (1 - core) + near * core
    return row, spot, level, core, first, second, 3 - row


def greet(levels, row, spot, level, core, first, second):
    barrier = pltpu.get_barrier_semaphore()
    above, below = level + 1 < levels, level >= 1
    sibling = spot + 1 - 2 * core

    def signal(device):
        pl.semaphore_signal(barrier, inc=1, device_id=device, device_id_type=MESH)

    signal({"dp": first, "seq": spot})
    signal({"dp": second, "seq": spot})
    signal({"dp": row, "seq": sibling})
    pl.when(above)(lambda: signal({"dp": row, "seq": spot + 2}))
    pl.when(below)(lambda: signal({"dp": row, "seq": spot - 2}))
    peers = 3 + (level + levels - 1) // levels + (2 * levels - 2 - level) // levels
    pl.semaphore_wait(barrier, peers)
    return above, below, sibling


class Sender:
    def __init__(self, semaphores):
        self.semaphores, self.used, self.pending = semaphores, 0, []

    def start(self, condition, source, target, device, arrival):
        copy = pltpu.make_async_remote_copy(
            src_ref=source, dst_ref=target, send_sem=self.semaphores.at[self.used], recv_sem=arrival,
            device_id=device, device_id_type=MESH,
        )
        self.used += 1
        when(condition, copy.start)
        self.pending.append((condition, copy))

    def arrived(self, condition, target, device, arrival):
        copy = pltpu.make_async_remote_copy(
            src_ref=target, dst_ref=target, send_sem=self.semaphores.at[0], recv_sem=arrival,
            device_id=device, device_id_type=MESH,
        )
        when(condition, copy.wait_recv)

    def drain(self):
        for condition, copy in self.pending:
            when(condition, copy.wait_send)


def gather_kernel(levels, share, full, by_level, by_first, by_second, by_core, sends, local):
    row, spot, level, core, first, second, both = place()
    above, below, sibling = greet(levels, row, spot, level, core, first, second)
    sender = Sender(sends)
    here = {"dp": first, "seq": spot}

    def piece(half, owner, owner_level):
        return full.at[owner, owner_level * 2 + core, half]

    def send(condition, half, owner, owner_level, device, arrival, own):
        target = piece(half, owner, owner_level)
        sender.start(condition, share.at[half] if own else target, target, device, arrival)

    def along(condition, up, half, side, owner, owner_level, own=False):
        device = {"dp": row, "seq": spot + 2 if up else spot - 2}
        send(condition, half, owner, owner_level, device, by_level.at[half, side, owner_level], own)

    def to_first(condition, half, owner_level, own=False):
        send(condition, half, row, owner_level, here, by_first.at[half, owner_level], own)

    def to_second(condition, half, side, owner, owner_level, own=False):
        device = {"dp": second, "seq": spot}
        send(condition, half, owner, owner_level, device, by_second.at[half, side, owner_level], own)

    def to_core(condition, half, owner, owner_level, own=False):
        device = {"dp": row, "seq": sibling}
        send(condition, half, owner, owner_level, device, by_core.at[half, owner, owner_level], own)

    def arrived(condition, half, owner, owner_level, arrival):
        sender.arrived(condition, piece(half, owner, owner_level), here, arrival)

    kept = [pltpu.make_async_copy(share.at[half], full.at[row, spot, half], local.at[half]) for half in range(2)]
    for copy in kept:
        copy.start()
    to_first(None, 1, level, True)
    along(above, True, 0, 0, row, level, True)
    along(below, False, 0, 0, row, level, True)
    to_second(None, 0, 0, row, level, True)
    to_first(None, 0, level, True)
    to_second(None, 1, 0, row, level, True)
    along(above, True, 1, 0, row, level, True)
    along(below, False, 1, 0, row, level, True)
    to_core(None, 0, row, level, True)
    to_core(None, 1, row, level, True)
    arrived(None, 1, first, level, by_first.at[1, level])
    along(above, True, 1, 1, first, level)
    along(below, False, 1, 1, first, level)
    to_second(None, 1, 1, first, level)
    to_core(None, 1, first, level)
    arrived(None, 0, first, level, by_first.at[0, level])
    to_second(None, 0, 1, first, level)
    to_core(None, 0, first, level)

    def from_second(condition, owner_level):
        for half in range(2):
            for side, owner in ((0, second), (1, both)):
                arrived(condition, half, owner, owner_level, by_second.at[half, side, owner_level])
                to_core(condition, half, owner, owner_level)

    waiting = [(None, level)]
    for step in range(1, levels):
        ways = ((level - step >= 0, level - step, True), (level + step < levels, level + step, False))

        def onward(up):
            if up:
                return (level - step >= 0) & above
            return (level + step < levels) & below

        for condition, source, up in ways:
            arrived(condition, 0, row, source, by_level.at[0, 0, source])
            if step < levels - 1:
                along(onward(up), up, 0, 0, row, source)
            to_first(condition, 0, source)
            to_second(condition, 0, 0, row, source)
            to_core(condition, 0, row, source)
        for side, owner in ((0, row), (1, first)):
            for condition, source, up in ways:
                arrived(condition, 1, owner, source, by_level.at[1, side, source])
                if step < levels - 1:
                    along(onward(up), up, 1, side, owner, source)
                to_second(condition, 1, side, owner, source)
                to_core(condition, 1, owner, source)
        for condition, source, up in ways:
            arrived(condition, 0, first, source, by_first.at[0, source])
            to_second(condition, 0, 1, first, source)
            to_core(condition, 0, first, source)
        for condition, source in waiting:
            from_second(condition, source)
        waiting = [(condition, source) for condition, source, _ in ways]
    for condition, source in waiting:
        from_second(condition, source)
    for half in range(2):
        for owner in range(4):
            for source in range(levels):
                target = full.at[owner, source * 2 + 1 - core, half]
                sender.arrived(None, target, here, by_core.at[half, owner, source])
    for copy in kept:
        copy.wait()
    sender.drain()


def gather(levels, share):
    dma = pltpu.SemaphoreType.DMA
    return pl.pallas_call(
        functools.partial(gather_kernel, levels),
        out_shape=jax.ShapeDtypeStruct((4, 2 * levels) + share.shape, share.dtype),
        in_specs=[pl.BlockSpec(memory_space=pl.ANY)],
        out_specs=pl.BlockSpec(memory_space=pl.ANY),
        scratch_shapes=[
            dma((2, 2, levels)),
            dma((2, levels)),
            dma((2, 2, levels)),
            dma((2, 4, levels)),
            dma((8 + 34 * levels,)),
            dma((2,)),
        ],
        compiler_params=pltpu.CompilerParams(collective_id=1, has_side_effects=True),
        name="gather_weights",
    )(share)


def scatter_kernel(
    levels, slots, grads, result, total, by_second, by_first, by_level, staged,
    core_sem, second_sem, first_sem, level_sem, load_sem, sends,
):
    row, spot, level, core, first, second, both = place()
    above, below, sibling = greet(levels, row, spot, level, core, first, second)
    sender = Sender(sends)
    here = {"dp": first, "seq": spot}
    width = grads.shape[-1]
    order = []
    for step in range((levels + 1) // 2):
        order += [levels - 1 - step] + ([step] if step < levels - 1 - step else [])

    def add(target, *others):
        def body(step, _):
            columns = pl.ds(pl.multiple_of(step * CHUNK, CHUNK), CHUNK)
            value = target[:, columns]
            for other in others:
                value = value + other[:, columns]
            target[:, columns] = value
            return 0

        lax.fori_loop(0, width // CHUNK, body, 0)

    def arrived(target, arrival):
        sender.arrived(None, target, here, arrival)

    away = [(end, half, side, owner) for end in order for half in (1, 0) for side, owner in ((0, second), (1, both))]
    stay = [(end, half, side, owner) for end in order for half in (1, 0) for side, owner in ((0, row), (1, first))]
    listed = away + stay
    for end, half, _, owner in listed:
        device = {"dp": row, "seq": sibling}
        source = grads.at[owner, end * 2 + 1 - core, half]
        sender.start(None, source, total.at[half, owner, end], device, core_sem.at[half, owner, end])

    def load(place_in_list):
        end, half, _, owner = listed[place_in_list]
        slot = place_in_list % slots
        return pltpu.make_async_copy(grads.at[owner, end * 2 + core, half], staged.at[slot], load_sem.at[slot])

    for slot in range(slots):
        load(slot).start()
    for number, (end, half, side, owner) in enumerate(listed):
        load(number).wait()
        sums = total.at[half, owner, end]
        arrived(sums, core_sem.at[half, owner, end])
        add(sums, staged.at[number % slots])
        if number + slots < len(listed):
            load(number + slots).start()
        if number < len(away):
            device = {"dp": second, "seq": spot}
            sender.start(None, sums, by_second.at[half, side, end], device, second_sem.at[half, side, end])

    def along(half, side, owner, end):
        sums = total.at[half, owner, end]

        def take(way):
            arrived(by_level.at[half, side, way, end], level_sem.at[half, side, way, end])
            add(sums, by_level.at[half, side, way, end])

        def pass_on(way, condition, has_more):
            pl.when(condition & has_more)(lambda: take(way))
            device = {"dp": row, "seq": spot + 2 if way == 0 else spot - 2}
            target = by_level.at[half, side, way, end]
            sender.start(condition, sums, target, device, level_sem.at[half, side, way, end])

        if end > 0:
            pass_on(0, level < end, below)
        if end < levels - 1:
            pass_on(1, level > end, above)

    def finish_first(end):
        sums = total.at[0, row, end]
        arrived(by_first.at[0, end], first_sem.at[0, end])
        add(sums, by_first.at[0, end])
        along(0, 0, row, end)

    previous = None
    for end in order:
        for side, owner in ((0, row), (1, first)):
            arrived(by_second.at[1, side, end], second_sem.at[1, side, end])
            add(total.at[1, owner, end], by_second.at[1, side, end])
            along(1, side, owner, end)
        for side, owner in ((1, first), (0, row)):
            sums = total.at[0, owner, end]
            arrived(by_second.at[0, side, end], second_sem.at[0, side, end])
            add(sums, by_second.at[0, side, end])
            if side == 1:
                sender.start(None, sums, by_first.at[0, end], here, first_sem.at[0, end])
        if previous is not None:
            finish_first(previous)
        previous = end
    finish_first(previous)

    def collect(half, side, owner):
        sums = total.at[half, owner, level]

        def take(way):
            arrived(by_level.at[half, side, way, level], level_sem.at[half, side, way, level])
            add(sums, by_level.at[half, side, way, level])

        pl.when(below)(lambda: take(0))
        pl.when(above)(lambda: take(1))

    def write(half, *parts):
        def body(step, _):
            columns = pl.ds(pl.multiple_of(step * CHUNK, CHUNK), CHUNK)
            value = parts[0][:, columns].astype(F32)
            for part in parts[1:]:
                value = value + part[:, columns].astype(F32)
            result[half, :, columns] = value
            return 0

        lax.fori_loop(0, width // CHUNK, body, 0)

    collect(1, 1, first)
    sender.start(None, total.at[1, first, level], by_first.at[1, 0], here, first_sem.at[1, 0])
    collect(1, 0, row)
    collect(0, 0, row)
    write(0, total.at[0, row, level])
    arrived(by_first.at[1, 0], first_sem.at[1, 0])
    write(1, total.at[1, row, level], by_first.at[1, 0])
    sender.drain()


def scatter(levels, grads):
    dma = pltpu.SemaphoreType.DMA
    piece = grads.shape[-2:]
    slots = 4
    return pl.pallas_call(
        functools.partial(scatter_kernel, levels, slots),
        out_shape=jax.ShapeDtypeStruct((2,) + piece, F32),
        in_specs=[pl.BlockSpec(memory_space=pl.ANY)],
        out_specs=pl.BlockSpec(memory_space=pltpu.VMEM),
        scratch_shapes=[
            pltpu.VMEM((2, 4, levels) + piece, BF16),
            pltpu.VMEM((2, 2, levels) + piece, BF16),
            pltpu.VMEM((2, levels) + piece, BF16),
            pltpu.VMEM((2, 2, 2, levels) + piece, BF16),
            pltpu.VMEM((slots,) + piece, BF16),
            dma((2, 4, levels)),
            dma((2, 2, levels)),
            dma((2, levels)),
            dma((2, 2, 2, levels)),
            dma((slots,)),
            dma((8 + 24 * levels,)),
        ],
        compiler_params=pltpu.CompilerParams(
            collective_id=2, has_side_effects=True, vmem_limit_bytes=58 * 2**20
        ),
        name="scatter_grads",
    )(grads)


def fits(rows):
    return lax.axis_size("dp") == 4 and lax.axis_size("seq") <= 16 and lax.axis_size("seq") % 2 == 0 and rows == 32


def gather_all(share):
    rows, width = share.shape
    if fits(rows):
        full = gather(lax.axis_size("seq") // 2, share.reshape(2, rows // 2, width))
        return full.reshape(-1, width)
    return lax.all_gather(share, ("dp", "seq"), axis=0, tiled=True)


def scatter_sum(grads):
    width = grads.shape[1]
    rows = grads.shape[0] // lax.axis_size(("dp", "seq"))
    if fits(rows):
        shaped = grads.reshape(lax.axis_size("dp"), lax.axis_size("seq"), 2, rows // 2, width)
        return scatter(lax.axis_size("seq") // 2, shaped).reshape(rows, width)
    return lax.psum_scatter(grads, ("dp", "seq"), scatter_dimension=0, tiled=True).astype(F32)


def pack_down(part):
    lead, tall = part.shape[:-2], part.shape[-2] // 11
    tiles = part.reshape(lead + (11, tall, 4, 2, 128))
    n = len(lead)
    moved = tiles.transpose(tuple(range(n)) + (n + 2, n + 1, n + 3, n, n + 4))
    return moved.reshape(lead + (4 * tall, FF))


def unpack_down(part):
    lead, tall = part.shape[:-2], part.shape[-2] // 4
    tiles = part.reshape(lead + (4, tall, 2, 11, 128))
    n = len(lead)
    moved = tiles.transpose(tuple(range(n)) + (n + 3, n + 1, n, n + 2, n + 4))
    return moved.reshape(lead + (11 * tall, MODEL_WIDTH))


def pack_small(mixer, mlp, beta, conv):
    rows = mixer.shape[0]
    taps = conv.reshape(KW, 3, rows).transpose(2, 0, 1).reshape(rows, 3 * KW)
    parts = jnp.concatenate([mixer[:, None], mlp[:, None], beta, taps], axis=1)
    return jnp.pad(parts, ((0, 0), (0, SMALL - parts.shape[1])))


def unpack_conv(small, rows):
    taps = small[:, CONV_AT : CONV_AT + 3 * KW].reshape(-1, rows, KW, 3)
    return taps.transpose(2, 0, 3, 1).reshape(KW, QKV)


def silu_slope(values):
    sigma = jax.nn.sigmoid(values)
    return sigma * (1.0 + values * (1.0 - sigma))


def norm_back(grad_in, values, inverse, gain):
    scaled = grad_in * gain
    return inverse * scaled - values * inverse**3 * jnp.mean(scaled * values, axis=-1, keepdims=True)


def dot(left, right, axes):
    return lax.dot_general(left, right, ((axes[:1], axes[1:]), ((), ())), preferred_element_type=F32)


def shards(
    tokens, cotangent, starts, mixer_gain, mix_weight, conv_weight, beta_weight, head_gain, out_weight, mlp_gain,
    upgate_weight, down_weight,
):
    rows, block, width = tokens.shape
    share_rows = mix_weight.shape[1]
    count = lax.axis_size("seq")
    halo = lax.ppermute(tokens[:, block - HALO :, :], "seq", [(k, k + 1) for k in range(count - 1)])
    halo = halo.reshape(rows * HALO, width)
    share = jnp.concatenate(
        [
            mix_weight[0],
            pack_small(mixer_gain[0], mlp_gain[0], beta_weight[0], conv_weight[0]),
            out_weight[0],
            upgate_weight[0],
            pack_down(down_weight[0]),
        ],
        axis=1,
    )
    full = gather_all(share)
    mix = full[:, :MIX]
    small = full[:, AT_SMALL:AT_OUT]
    out_w = full[:, AT_OUT:AT_UP]
    upgate_w = full[:, AT_UP:AT_DOWN]
    down_w = unpack_down(full[:, AT_DOWN:].reshape(-1, share_rows, FF)).reshape(FF, width)
    conv = unpack_conv(small, share_rows).astype(F32)
    mixer_g = small[:, 0].astype(F32)[None]
    mlp_g = small[:, 1].astype(F32)[None]
    head_f = head_gain.astype(F32)

    flat = tokens.reshape(rows * block, width)
    normed, pre, raw, beta, solved, solved_w, fresh, state, power, outputs, gated = mixer_forward(
        starts, flat, halo, mixer_g, mix, small, conv, head_f
    )
    hidden_mid = flat.astype(F32) + dot(gated, out_w, (1, 0))
    inverse_mid = lax.rsqrt(jnp.mean(hidden_mid * hidden_mid, axis=-1, keepdims=True) + NEAR_ZERO)
    normed_mid = (hidden_mid * inverse_mid * mlp_g).astype(BF16)
    upgate = dot(normed_mid, upgate_w, (1, 0))
    gate_part, up_part = upgate[:, :FF], upgate[:, FF:]
    acted = (jax.nn.silu(gate_part) * up_part).astype(BF16)
    output = (hidden_mid + dot(acted, down_w, (1, 0))).astype(BF16)

    down_grad = cotangent.reshape(rows * block, width)
    grad = down_grad.astype(F32)
    grad_down_w = dot(acted, down_grad, (0, 0)).astype(BF16)
    grad_acted = dot(down_grad, down_w, (1, 1))
    grad_upgate = jnp.concatenate(
        [grad_acted * up_part * silu_slope(gate_part), grad_acted * jax.nn.silu(gate_part)], axis=-1
    ).astype(BF16)
    grad_upgate_w = dot(normed_mid, grad_upgate, (0, 0)).astype(BF16)
    grad_normed_mid = dot(grad_upgate, upgate_w, (1, 1))
    grad_mlp_g = jnp.sum(grad_normed_mid * hidden_mid * inverse_mid, axis=0)
    grad_mid = grad + norm_back(grad_normed_mid, hidden_mid, inverse_mid, mlp_g)
    attn_grad = grad_mid.astype(BF16)
    grad_out_w = dot(gated, attn_grad, (0, 0)).astype(BF16)
    grad_gated = dot(attn_grad, out_w, (1, 1))

    grad_hidden, grad_project, grad_logits, grad_conv, grad_head, grad_mixer_g = mixer_backward(
        starts, grad_gated, grad_mid, flat, mixer_g, mix, small, conv, head_f,
        pre, raw, beta, solved, solved_w, fresh, state, power, outputs,
    )
    head_sum = lax.psum(jnp.sum(grad_head, axis=0, keepdims=True), ("dp", "seq"))
    grad_mix_w = dot(normed, grad_project, (0, 0)).astype(BF16)
    grad_beta_w = dot(normed, grad_logits, (0, 0))[:, BETA_AT:CONV_AT]
    taps = grad_conv.reshape(KW, -1, 3, share_rows).transpose(1, 3, 0, 2).reshape(width, 3 * KW)
    grad_small = jnp.concatenate([grad_mixer_g.T, grad_mlp_g[:, None], grad_beta_w, taps], axis=1)
    grad_small = jnp.pad(grad_small, ((0, 0), (0, SMALL - grad_small.shape[1]))).astype(BF16)
    packed = jnp.concatenate(
        [
            grad_mix_w,
            grad_small,
            grad_out_w,
            grad_upgate_w,
            pack_down(grad_down_w.reshape(-1, share_rows * FF // width, width)).reshape(width, FF),
        ],
        axis=1,
    )
    mine = scatter_sum(packed)
    conv_mine = mine[:, AT_SMALL + CONV_AT : AT_SMALL + CONV_AT + 3 * KW]
    conv_mine = conv_mine.reshape(share_rows, KW, 3).transpose(1, 2, 0).reshape(1, KW, 3 * share_rows)
    return (
        output.reshape(rows, block, width),
        grad_hidden.reshape(rows, block, width),
        mine[:, AT_SMALL][None],
        mine[:, :MIX][None],
        conv_mine,
        mine[:, AT_SMALL + BETA_AT : AT_SMALL + CONV_AT][None],
        head_sum,
        mine[:, AT_OUT:AT_UP][None],
        mine[:, AT_SMALL + 1][None],
        mine[:, AT_UP:AT_DOWN][None],
        unpack_down(mine[:, AT_DOWN:])[None],
    )


def solution(mesh):
    both = ("dp", "seq")
    in_specs = (
        P("dp", "seq", None),
        P("dp", "seq", None),
        P("dp", None),
        P(None, both),
        P(None, both, None),
        P(None, None, both),
        P(None, both, None),
        P(),
        P(None, both, None),
        P(None, both),
        P(None, both, None),
        P(None, both, None),
    )
    out_specs = (
        P("dp", "seq", None),
        P("dp", "seq", None),
        P(None, both),
        P(None, both, None),
        P(None, None, both),
        P(None, both, None),
        P(),
        P(None, both, None),
        P(None, both),
        P(None, both, None),
        P(None, both, None),
    )
    return jax.shard_map(shards, mesh=mesh, in_specs=in_specs, out_specs=out_specs, check_vma=False)
```

time: 1880 us -> 510 us (0.27)
  waiting for transfers between devices: 985 us -> 0.01 us
  Pallas kernels: 0 us -> 342 us
  matrix products: 267 us -> 45.5 us
  other arithmetic: 221 us -> 4.64 us
  local copies, waits for them, and re-layouts: 179 us -> 66.8 us
  blocking collectives: 139 us -> 46.4 us
  starting transfers between devices: 58.7 us -> 2.35 us
    reduce_scatter x4 -> x0, waiting for transfers between devices: 742 us -> none  [the longest x1 253 us: shards(): lax.psum_scatter(terms[6], ('dp', 'seq'), scatter_dimension=0, tiled=True)]
    pallas_call x0 -> x4, Pallas kernels: none -> 342 us  [the longest x1 131 us: scatter(): pl.pallas_call(functools.partial(scatter_kernel, levels, slots), out_shap...]
    dot_general x91 -> x11, matrix products: 242 us -> 45.5 us  [dot(): lax.dot_general(left, right, ((axes[:1], axes[1:]), ((), ())), preferred_...]
    another operation x20 -> x1, other arithmetic: 169 us -> 0.01 us  [the longest x5 158 us: block_parts(): jax.scipy.linalg.solve_triangular(system, weighted * keys_in, lower=True,...]
    ppermute x10 -> x1, waiting for transfers between devices: 158 us -> 0.01 us  [shards(): lax.ppermute(tokens[:, block - HALO:, :], 'seq', [(k, k + 1) for k in ran...]
    all_gather x2 -> x0, blocking collectives: 96.8 us -> none  [the longest x1 57.3 us: shards(): lax.all_gather(conv_weight[layer_index], ('dp', 'seq'), axis=1, tiled=True)]
    psum x1 -> x0, waiting for transfers between devices: 83.5 us -> none  [shards(): lax.psum((small_stack[0], small_stack[1], small_stack[2], small_stack[3],...]
    ppermute x10 -> x1, starting transfers between devices: 58.1 us -> 2.35 us  [shards(): lax.ppermute(tokens[:, block - HALO:, :], 'seq', [(k, k + 1) for k in ran...]
  transfers between devices with their start and end apart: 19 -> 1, of which waited for: 14 -> 0; matrix products, arithmetic and copies ran while one was open for 23% -> 6% of each run, Pallas kernels for 0% -> 22%
where the time goes in v1:
time: 510 us; the launch traced here: 509 us
  Pallas kernels  342 us (67%)
  local copies, waits for them, and re-layouts  66.8 us (13%)
  blocking collectives  46.4 us (9%)
  matrix products  45.5 us (9%)
    pallas_call x1, Pallas kernels, scatter(): pl.pallas_call(functools.partial(scatter_kernel, levels, slots), out_shap...  131 us
    pallas_call x1, Pallas kernels, gather(): pl.pallas_call(functools.partial(gather_kernel, levels), out_shape=jax.Sh...  111 us
    pallas_call x1, Pallas kernels, mixer_backward(): pl.pallas_call(mixer_backward_kernel, out_shape=[shape((ALL, MODEL_WIDTH)...  62.1 us
    psum x1, blocking collectives, shards(): lax.psum(jnp.sum(grad_head, axis=0, keepdims=True), ('dp', 'seq'))  46.4 us
    dot_general x11, matrix products, dot(): lax.dot_general(left, right, ((axes[:1], axes[1:]), ((), ())), preferred_...  45.5 us
    pallas_call x1, Pallas kernels, mixer_forward(): pl.pallas_call(mixer_forward_kernel, out_shape=[shape((ALL, MODEL_WIDTH),...  38.7 us
    unnamed x40, local copies, waits for them, and re-layouts  25.7 us
  transfers between devices with their start and end apart: 1, of which 0 were waited for; matrix products, arithmetic and copies ran while one was open for 6% of the time, Pallas kernels for 22%

profile of v1, /device:TPU:0, one launch (start us, length us, event | category | flops | bytes accessed | tf_op | source)
XLA Modules:
  0.0 508.9 jit_solution(17947196469942320558)
XLA Ops:
  1.4 2.3 collective-permute-start
  10.1 110.6 %gather_weights.1 = bf16[4,8,2,16,13824]{4,3,2,1,0:T(8,128)(2,1)} custom-call(bf16[2,16,13824]{2,1,0:T(8,128)(2,1)} %copy-done.5), custom_call_target="tpu_custom_call" | custom-call | tf_op jit(solution)/shard_map/gather_weights/pallas_call | solution.py:755
  121.9 1.9 convert_reduce_fusion
  123.8 7.8 %slice.85.mix = bf16[1024,4096]{1,0:T(8,128)(2,1)} slice(bf16[1024,13824]{1,0:T(8,128)(2,1)} %bitcast.78), slice={[0:1024], [0:4096]} | slice | bytes 16777216 | tf_op jit(solution)/shard_map/slice | solution.py:1010
  133.5 5.5 %slice.93 = bf16[1024,2816]{1,0:T(8,128)(2,1)} slice(bf16[1024,13824]{1,0:T(8,128)(2,1)} %bitcast.80), slice={[0:1024], [11008:13824]} | slice | bytes 11534336 | tf_op jit(solution)/shard_map/slice | solution.py:1014
  140.7 4.2 copy.51
  145.7 38.7 %mixer_forward.1 = (bf16[256,1024]{1,0:T(8,128)(2,1)}, f32[272,4096]{1,0:T(8,128)}, f32[256,3072]{1,0:T(8,128)}, f32[256,256]{1,0:T(8,128)}, bf16[8,256,256]{2,1...) custom-call(s32[2,4]{1,0:T(2,128)} %starts.3, ...), custom_call_target="tpu_custom_call" | custom-call | tf_op jit(solution)/shard_map/mixer_forward/pallas_call | solution.py:298
  184.4 2.6 multiply_reduce_fusion.2
  187.0 6.2 %fusion.2 = f32[256,5632]{1,0:T(8,128)S(1)} fusion(bf16[1024,13824]{1,0:T(8,128)(2,1)} %bitcast.82, f32[256,1024]{1,0:T(8,128)S(1)} %get-tuple-element.57, f32[1024]{0:T(1024)S(1)} %get-tuple-element.45, f32[256]{0:T(256)S(1)} %get-tuple-element.55), kind=kOutput, calls=%fused_computation.3 | convolution fusion | flops 2953576448 | bytes 18355200 | tf_op jit(solution)/shard_map/dot_general | solution.py:987
  193.2 2.9 multiply_convert_fusion.1
  196.1 6.3 %multiply_reduce_fusion = (bf16[1024]{0:T(1024)(128)(2,1)S(1)}, f32[256]{0:T(256)S(1)}, f32[256,1024]{1,0:T(8,128)S(1)}) fusion(f32[256,1024]{1,0:T(8,128)S(1)} %get-tuple-element.57, f32[256]{0:T(256)S(1)} %get-tuple-element.55, f32[1024]{0:T(1024)S(1)} %get-tuple-element.45, bf16[1024,13824]{1,0:T(8,128)(2,1)} %bitcast.83, ...), kind=kOutput, calls=%fused_computation.22 | convolution fusion | flops 2960128768 | bytes 16523264 | tf_op jit(solution)/shard_map/dot_general | solution.py:987
  202.8 3.7 fusion.5.grad_gated
  207.2 6.3 %convolution_convert_fusion = bf16[1024,5632]{1,0:T(8,128)(2,1)} fusion(bf16[256,2816]{1,0:T(8,128)(2,1)S(1)} %get-tuple-element.52, bf16[256,2816]{1,0:T(8,128)(2,1)S(1)} %get-tuple-element.51, f32[256,1024]{1,0:T(8,128)S(1)} %get-tuple-element.57, f32[1024]{0:T(1024)S(1)} %get-tuple-element.45, f32[256]{0:T(256)S(1)} %get-tuple-element.55), kind=kOutput, calls=%fused_computation | convolution fusion | flops 2965110784 | bytes 15471616 | tf_op jit(solution)/shard_map/dot_general | solution.py:987
  213.5 5.1 fusion.12
  218.6 4.1 convolution_convert_fusion.2
  222.7 62.1 %mixer_backward.1 = (f32[256,1024]{1,0:T(8,128)}, bf16[256,4096]{1,0:T(8,128)(2,1)}, bf16[256,256]{1,0:T(8,128)(2,1)}, f32[4,3072]{1,0:T(4,128)}, f32[8,128]{1,0:T(8,128)}, /*index=5*/f32[1,1024]{1,0:T(1,128)}) custom-call(s32[2,4]{1,0:T(2,128)} %starts.3, f32[256,1024]{1,0:T(8,128)} %fusion.5.grad_gated, f32[256,1024]{1,0:T(8,128)} %copy-done, ...), custom_call_target="tpu_custom_call" | custom-call | tf_op jit(solution)/shard_map/mixer_backward/pallas_call | solution.py:560
  284.8 7.3 %convolution_convert_fusion.1 = bf16[1024,4096]{1,0:T(8,128)(2,1)} fusion(bf16[256,1024]{1,0:T(8,128)(2,1)S(1)} %copy-done.3, bf16[256,4096]{1,0:T(8,128)(2,1)} %get-tuple-element.40), kind=kOutput, calls=%fused_computation.5 | convolution fusion | flops 2151677952 | bytes 11010048 | tf_op jit(solution)/shard_map/dot_general | solution.py:987
  292.1 7.8 %constant_dynamic-update-slice_fusion.9 = bf16[4,8,2,16,13824]{4,3,2,1,0:T(8,128)(2,1)} fusion(bf16[4,8,2,16,4096]{4,3,2,1,0:T(8,128)(2,1)} %bitcast.87), kind=kLoop, calls=%fused_computation.46 | loop fusion | bytes 16777216
  301.0 3.6 copy.55
  307.0 9.1 %constant_dynamic-update-slice_fusion.6 = bf16[4,8,2,16,13824]{4,3,2,1,0:T(8,128)(2,1)} fusion(bf16[4,8,2,16,13824]{4,3,2,1,0:T(8,128)(2,1)} %constant_dynamic-update-slice_fusion.7, bf16[4,8,2,16,5632]{4,3,2,1,0:T(8,128)(2,1)} %bitcast.85), kind=kLoop, calls=%fused_computation.43 | loop fusion | bytes 23068672
  316.1 2.8 constant_dynamic-update-slice_fusion.5.grads
  319.0 130.8 %scatter_grads.1 = f32[2,16,13824]{2,1,0:T(8,128)} custom-call(bf16[4,8,2,16,13824]{4,3,2,1,0:T(8,128)(2,1)} %constant_dynamic-update-slice_fusion.5.grads), custom_call_target="tpu_custom_call" | custom-call | tf_op jit(solution)/shard_map/scatter_grads/pallas_call | solution.py:902
  456.3 2.0 slice_bitcast_fusion
  460.8 46.4 %psum.7 = f32[1,128]{1,0:T(1,128)} all-reduce(f32[1,128]{1,0:T(1,128)S(1)} %bitcast.126), channel_id=1, replica_groups=mesh['dp'=4,'seq'=8] {'dp','seq'}, use_global_device_ids=true, to_apply=%region_4.5 | all-reduce | flops 128 | bytes 1024 | tf_op jit(solution)/shard_map/psum | solution.py:1051
  (78 shorter events, 27.6 us)
Async XLA Ops:
  1.4 143.6 %collective-permute-start = (bf16[2,8,1024]{2,1,0:T(8,128)(2,1)S(1)}, bf16[2,8,1024]{2,1,0:T(8,128)(2,1)S(1)}, u32[]{:S(2)}, u32[]{:S(2)}) collective-permute-start(bf16[2,8,1024]{2,1,0:T(8,128)(2,1)S(1)} %slice.64), channel_id=1, source_target_pairs={{0,1},{1,2},{2,3},{3,4},{4,5},{5,6},{6,7},{8,9},{9,10},{10,11},{11... | collective-permute-start | bytes 98312 | tf_op jit(solution)/shard_map/ppermute | solution.py:997
  9.2 0.9 copy-start.5
  133.5 6.7 %copy-start.13 = (bf16[1,128]{1,0:T(2,128)(2,1)S(1)}, bf16[1,128]{1,0:T(2,128)(2,1)}, u32[]{:S(2)}) copy-start(bf16[1,128]{1,0:T(2,128)(2,1)} %param.19) | copy-start | bytes 772
  145.0 48.2 %copy-start.1 = (bf16[32,4,8,2,11,128]{5,2,3,1,4,0:T(8,128)(2,1)}, bf16[32,4,8,2,11,128]{5,2,3,1,4,0:T(8,128)(2,1)S(1)}, u32[]{:S(2)}) copy-start(bf16[32,4,8,2,11,128]{5,2,3,1,4,0:T(8,128)(2,1)S(1)} %copy.51) | copy-start | bytes 17301508
  145.0 0.7 copy-start.10
  145.7 38.7 %copy-start.2 = (bf16[2,128,1024]{2,1,0:T(8,128)(2,1)S(1)}, bf16[2,128,1024]{2,1,0:T(8,128)(2,1)}, u32[]{:S(2)}) copy-start(bf16[2,128,1024]{2,1,0:T(8,128)(2,1)} %param.12) | copy-start | bytes 1572868
  187.0 6.2 %copy-start.4 = (bf16[2,128,1024]{2,1,0:T(8,128)(2,1)S(1)}, bf16[2,128,1024]{2,1,0:T(8,128)(2,1)}, u32[]{:S(2)}) copy-start(bf16[2,128,1024]{2,1,0:T(8,128)(2,1)} %param.13) | copy-start | bytes 1572868
  202.4 4.0 copy-start.7
  202.7 10.7 %copy-start = (f32[256,1024]{1,0:T(8,128)}, f32[256,1024]{1,0:T(8,128)S(1)}, u32[]{:S(2)}) copy-start(f32[256,1024]{1,0:T(8,128)S(1)} %subtract_add_fusion.grad_mid) | copy-start | bytes 3145732
  222.7 62.1 %copy-start.3 = (bf16[256,1024]{1,0:T(8,128)(2,1)S(1)}, bf16[256,1024]{1,0:T(8,128)(2,1)}, u32[]{:S(2)}) copy-start(bf16[256,1024]{1,0:T(8,128)(2,1)} %get-tuple-element.39) | copy-start | bytes 1572868
  292.1 7.8 %copy-start.9 = (f32[4,3072]{1,0:T(4,128)S(1)}, f32[4,3072]{1,0:T(4,128)}, u32[]{:S(2)}) copy-start(f32[4,3072]{1,0:T(4,128)} %get-tuple-element.43) | copy-start | bytes 147460
  292.1 8.2 %copy-start.8 = (bf16[256,256]{1,0:T(8,128)(2,1)S(1)}, bf16[256,256]{1,0:T(8,128)(2,1)}, u32[]{:S(2)}) copy-start(bf16[256,256]{1,0:T(8,128)(2,1)} %get-tuple-element.42) | copy-start | bytes 393220
  292.1 8.5 %copy-start.12 = (f32[1,1024]{1,0:T(1,128)S(1)}, f32[1,1024]{1,0:T(1,128)}, u32[]{:S(2)}) copy-start(f32[1,1024]{1,0:T(1,128)} %get-tuple-element.41) | copy-start | bytes 12292
  319.0 141.8 %copy-start.11 = (f32[8,128]{1,0:T(8,128)S(1)}, f32[8,128]{1,0:T(8,128)}, u32[]{:S(2)}) copy-start(f32[8,128]{1,0:T(8,128)} %get-tuple-element.44) | copy-start | bytes 12292
  449.7 58.2 %copy-start.6 = (f32[256,1024]{1,0:T(8,128)S(1)}, f32[256,1024]{1,0:T(8,128)}, u32[]{:S(2)}) copy-start(f32[256,1024]{1,0:T(8,128)} %get-tuple-element.38) | copy-start | bytes 3145732
